TPU v7x, 32 devices: a whole 2x2x4 slice. The times are simulated.
32 devices in a mesh: dp: 8 (over z, x), mp: 4 (over y, core).
Axes of the slice: x: 2, y: 2, z: 4, core: 2. Of those that a mesh axis runs over, the one named last changes fastest.
Arguments:
- hidden_in: bfloat16 [16384, 768], P(('dp', 'mp')), may hold values from -6 to 6
- image_feats: bfloat16 [256, 257, 1408], P('dp'), may hold values from -6 to 6
- caption_lengths: int32 [256], P('dp'), may hold values from 5 to 32, as said below
- out_grad: bfloat16 [16384, 768], P(('dp', 'mp')), may hold values from -6 to 6
- proj_in: float32 [4, 768, 768], P(None, 'dp', 'mp')
- proj_in_moments: float32 [2, 4, 768, 768], P(None, None, 'dp', 'mp')
- proj_in_average: float32 [4, 768, 768], P(None, 'dp', 'mp')
- proj_out: float32 [2, 768, 768], P(None, ('mp', 'dp'))
- proj_out_moments: float32 [2, 2, 768, 768], P(None, None, ('mp', 'dp'))
- proj_out_average: float32 [2, 768, 768], P(None, ('mp', 'dp'))
- image_kv: float32 [2, 1408, 768], P(None, 'dp', 'mp')
- image_kv_moments: float32 [2, 2, 1408, 768], P(None, None, 'dp', 'mp')
- image_kv_average: float32 [2, 1408, 768], P(None, 'dp', 'mp')
- feed_up: float32 [768, 3072], P('dp', 'mp')
- feed_up_moments: float32 [2, 768, 3072], P(None, 'dp', 'mp')
- feed_up_average: float32 [768, 3072], P('dp', 'mp')
- feed_down: float32 [3072, 768], P(('mp', 'dp'))
- feed_down_moments: float32 [2, 3072, 768], P(None, ('mp', 'dp'))
- feed_down_average: float32 [3072, 768], P(('mp', 'dp'))
- norm_params: float32 [6, 768], P(None, ('mp', 'dp'))
- norm_params_moments: float32 [2, 6, 768], P(None, None, ('mp', 'dp'))
- norm_params_average: float32 [6, 768], P(None, ('mp', 'dp'))
Outputs:
- block_out: bfloat16 [16384, 768], P(('dp', 'mp'))
- input_grad: bfloat16 [16384, 768], P(('dp', 'mp'))
- new_proj_in: float32 [4, 768, 768], P(None, 'dp', 'mp')
- new_proj_in_moments: float32 [2, 4, 768, 768], P(None, None, 'dp', 'mp')
- new_proj_in_average: float32 [4, 768, 768], P(None, 'dp', 'mp')
- new_proj_out: float32 [2, 768, 768], P(None, ('mp', 'dp'))
- new_proj_out_moments: float32 [2, 2, 768, 768], P(None, None, ('mp', 'dp'))
- new_proj_out_average: float32 [2, 768, 768], P(None, ('mp', 'dp'))
- new_image_kv: float32 [2, 1408, 768], P(None, 'dp', 'mp')
- new_image_kv_moments: float32 [2, 2, 1408, 768], P(None, None, 'dp', 'mp')
- new_image_kv_average: float32 [2, 1408, 768], P(None, 'dp', 'mp')
- new_feed_up: float32 [768, 3072], P('dp', 'mp')
- new_feed_up_moments: float32 [2, 768, 3072], P(None, 'dp', 'mp')
- new_feed_up_average: float32 [768, 3072], P('dp', 'mp')
- new_feed_down: float32 [3072, 768], P(('mp', 'dp'))
- new_feed_down_moments: float32 [2, 3072, 768], P(None, ('mp', 'dp'))
- new_feed_down_average: float32 [3072, 768], P(('mp', 'dp'))
- new_norm_params: float32 [6, 768], P(None, ('mp', 'dp'))
- new_norm_params_moments: float32 [2, 6, 768], P(None, None, ('mp', 'dp'))
- new_norm_params_average: float32 [6, 768], P(None, ('mp', 'dp'))
- trust_ratios: float32 [16], replicated
- norm_values: float32 [2, 16], replicated
Inputs may be any that keep to these rules, and one draw needn't show every extreme that they name: `caption_lengths`: in every draw some caption has 32 tokens and some has 5.
All inputs are finite; a program needn't handle non-finite values.
Results may differ from a plain program's by a relative error of at most 0.025.
The roundings to bfloat16 on the way count: a program that leaves them out, or rounds other values in their place, can miss the bound.
Values may be sent and summed in bfloat16 or wider, within the bound.
No kernel may reach another device: no remote copies, remote signals or barrier semaphores. Data moves between devices by JAX's collectives and lax.ppermute only.
A program may use at most 192 MiB of HBM per device.

v0:
```python
import functools

import jax
import jax.numpy as jnp
from jax import lax
from jax.experimental import pallas as pl
from jax.experimental.pallas import tpu as pltpu
from jax.sharding import PartitionSpec as P

HEAD = 64
PATCHES = 257
QUERIES = 32
TEXT = 32
SEQ = QUERIES + TEXT
STEP = 10


NORM_EPSILON = 1e-06
ADAM_EPSILON = 1e-06
SQUARE_EPSILON = 1e-06
BETA_ONE = 0.9
BETA_TWO = 0.999
LEARN_RATE = 0.5
DECAY_RATE = 0.01
AVERAGE_RATE = 0.6
MASK_VALUE = -1e30

AXES = ("dp", "mp")
GROUPS = 8
MODEL = 4
SLOTS = 16
NORM_ROWS = 8
LANES = 128
IMAGE_SPLIT = 64
SELF_SPLIT = 48
BLOCK = 128
WIDE = 256
HEADS_AT_ONCE = 12
SLOT = 272
MIB = 1024 * 1024

BF16 = jnp.bfloat16
F32 = jnp.float32


def dot_nn(left_side, right_side):
    return lax.dot_general(
        left_side, right_side, (((1,), (0,)), ((), ())), preferred_element_type=F32
    )


def dot_nt(left_side, right_side):
    return lax.dot_general(
        left_side, right_side, (((1,), (1,)), ((), ())), preferred_element_type=F32
    )


def dot_tn(left_side, right_side):
    return lax.dot_general(
        left_side, right_side, (((0,), (0,)), ((), ())), preferred_element_type=F32
    )


def normalise(inputs):
    centred = inputs - jnp.mean(inputs, axis=-1, keepdims=True)
    inverse = lax.rsqrt(jnp.mean(centred * centred, axis=-1, keepdims=True) + NORM_EPSILON)
    return centred * inverse, inverse


def norm_back(gradient, normed, inverse, gain):
    scaled = gradient * gain
    centre_term = jnp.mean(scaled, axis=-1, keepdims=True)
    normed_term = jnp.mean(scaled * normed, axis=-1, keepdims=True)
    return inverse * (scaled - centre_term - normed * normed_term)


def slot_of(place, block, y_rel):
    return place[block] * 8 + y_rel * 4 + place[GROUPS + block]


def softmax(scores):
    tops = [jnp.max(each, axis=-1, keepdims=True) for each in scores]
    exponents = [jnp.exp(each - top) for each, top in zip(scores, tops)]
    totals = [jnp.sum(each, axis=-1, keepdims=True) for each in exponents]
    return [each / total for each, total in zip(exponents, totals)]


def block_mask(lengths, first_item):
    per_block = BLOCK // SEQ
    row = lax.broadcasted_iota(jnp.int32, (BLOCK, BLOCK), 0)
    column = lax.broadcasted_iota(jnp.int32, (BLOCK, BLOCK), 1)
    row_item, column_item = lax.shift_right_logical(row, 6), lax.shift_right_logical(column, 6)
    slot = column - column_item * SEQ
    limit = jnp.zeros((BLOCK, BLOCK), jnp.int32)
    for item in range(per_block):
        limit = jnp.where(column_item == item, lengths[first_item + item] + QUERIES, limit)
    return (row_item == column_item) & (slot < limit)


def self_forward_kernel(
    place,
    lengths,
    hidden,
    begin_own,
    begin_other,
    first_in,
    qkv,
    heads,
    w_qkv,
    w_cross,
    w_self_out,
    w_cross_out,
    norm,
    self_rows,
    cross_rows,
):
    rows, features = hidden.shape
    width = features // MODEL
    block_rows = features // GROUPS
    out_rows = width // GROUPS
    half, part = block_rows // 2, begin_own.shape[1] // 2
    norm_sum = jnp.zeros((NORM_ROWS, features), F32)
    for block in range(GROUPS):
        pieces = []
        for model in range(MODEL):
            side, y_rel = divmod(model, 2)
            source, slot = (begin_own, begin_other)[side], slot_of(place, block, y_rel)
            pieces.append(
                jnp.concatenate(
                    [source[slot, :half, :], source[slot, part : part + half, :]], axis=0
                )
            )
            cross_part = source[slot, half:part, :].astype(F32)
            self_part = source[slot, part + half :, :].astype(F32)
            begin = model * width + block * out_rows
            cross_rows[begin : begin + out_rows, :] = cross_part[:out_rows]
            self_rows[begin : begin + out_rows, :] = self_part[:out_rows]
            norm_sum = norm_sum + self_part[out_rows:]
        begin = block * block_rows
        for kind in range(4):
            joined = jnp.concatenate(
                [piece[:, kind * width : (kind + 1) * width] for piece in pieces], axis=1
            )
            if kind < 3:
                w_qkv[begin : begin + block_rows, kind * features : (kind + 1) * features] = joined
            else:
                w_cross[begin : begin + block_rows, :] = joined
    norm[...] = norm_sum
    w_self_out[...] = self_rows[...].astype(BF16)
    w_cross_out[...] = cross_rows[...].astype(BF16)
    tokens = hidden[...]
    for kind in range(3):
        columns = slice(kind * features, (kind + 1) * features)
        qkv[:, columns] = dot_nn(tokens, w_qkv[:, columns]).astype(BF16)
    scale = HEAD ** (-0.5)
    for begin in range(0, rows, BLOCK):
        span = slice(begin, begin + BLOCK)
        mask = block_mask(lengths, begin // SEQ)
        for first in range(0, features // HEAD, HEADS_AT_ONCE):
            queries, key_rows, value_rows = [
                [
                    qkv[span, kind * features + head * HEAD : kind * features + (head + 1) * HEAD]
                    for head in range(first, first + HEADS_AT_ONCE)
                ]
                for kind in range(3)
            ]
            scores = [dot_nt(*pair) for pair in zip(queries, key_rows)]
            probs = softmax([jnp.where(mask, each * scale, MASK_VALUE) for each in scores])
            mixed = [dot_nn(*pair) for pair in zip([each.astype(BF16) for each in probs], value_rows)]
            heads[span, first * HEAD : (first + HEADS_AT_ONCE) * HEAD] = jnp.concatenate(
                [each.astype(BF16) for each in mixed], axis=1
            )
    first_in[...] = tokens.astype(F32) + dot_nn(heads[...], w_self_out[...])


def assemble_image(place, image_own, image_other, weight):
    block_rows = image_own.shape[1]
    width = image_own.shape[2] // 2
    features = width * MODEL
    for block in range(GROUPS):
        pieces = []
        for model in range(MODEL):
            side, y_rel = divmod(model, 2)
            pieces.append((image_own, image_other)[side][slot_of(place, block, y_rel)])
        begin = block * block_rows
        for kind in range(2):
            weight[begin : begin + block_rows, kind * features : (kind + 1) * features] = (
                jnp.concatenate(
                    [piece[:, kind * width : (kind + 1) * width] for piece in pieces], axis=1
                )
            )


def head_rows(values, head_mask):
    stacked = jnp.concatenate([values] * (WIDE // HEAD), axis=0)
    return jnp.where(head_mask, stacked, jnp.zeros_like(stacked))


def fold_heads(values, head_mask):
    kept = jnp.where(head_mask, values, 0.0)
    count = WIDE // HEAD
    size = values.shape[0] // count
    total = kept[:size]
    for index in range(1, count):
        total = total + kept[index * size : (index + 1) * size]
    return total


def query_head_mask():
    shape = (QUERIES * (WIDE // HEAD), WIDE)
    row = lax.broadcasted_iota(jnp.int32, shape, 0)
    column = lax.broadcasted_iota(jnp.int32, shape, 1)
    return lax.shift_right_logical(row, 5) == lax.shift_right_logical(column, 6)


def patch_softmax(queries, keys):
    scores = [dot_nt(*pair) * HEAD ** (-0.5) for pair in zip(queries, keys)]
    column = lax.broadcasted_iota(jnp.int32, scores[0].shape, 1)
    return softmax([jnp.where(column < PATCHES, each, MASK_VALUE) for each in scores])


def query_rows(values):
    items = values.shape[0] // SEQ
    return jnp.concatenate(
        [values[item * SEQ : item * SEQ + QUERIES] for item in range(items)], axis=0
    )


def look_kernel(
    place,
    feats,
    image_own,
    image_other,
    first_in,
    norm,
    w_cross,
    w_cross_out,
    key_values,
    second_in,
    queries,
    heads,
    weight,
):
    features = first_in.shape[1]
    patches = feats.shape[1]
    step, steps = pl.program_id(0), pl.num_programs(0)

    @pl.when(step == 0)
    def _():
        assemble_image(place, image_own, image_other, weight)
        normed, _ = normalise(query_rows(first_in[...]))
        one_query = normed * norm[0:1, :] + norm[1:2, :]
        second_in[...] = one_query
        queries[...] = dot_nn(one_query.astype(BF16), w_cross[...]).astype(BF16)

    key_values[:patches, :] = dot_nn(feats[0], weight[...]).astype(BF16)
    key_values[patches:, :] = jnp.zeros((SLOT - patches, weight.shape[1]), BF16)
    head_mask = query_head_mask()
    span = pl.ds(pl.multiple_of(step * QUERIES, QUERIES), QUERIES)
    columns = [slice(begin, begin + WIDE) for begin in range(0, features, WIDE)]
    value_columns = [slice(features + each.start, features + each.stop) for each in columns]
    expanded = [head_rows(queries[span, each], head_mask) for each in columns]
    probs = patch_softmax(expanded, [key_values[:, each] for each in columns])
    mixed = [
        dot_nn(prob.astype(BF16), key_values[:, each]) for prob, each in zip(probs, value_columns)
    ]
    for each, values in zip(columns, mixed):
        heads[span, each] = fold_heads(values, head_mask).astype(BF16)

    @pl.when(step == steps - 1)
    def _():
        second_in[...] += dot_nn(heads[...], w_cross_out[...])


def gelu_cumulative(inputs):
    return 0.5 * (1.0 + lax.erf(inputs * 0.7071067811865476))


def feed_kernel(
    place,
    lengths,
    norm,
    first_hbm,
    second_hbm,
    out_grad_hbm,
    up_first,
    down_first,
    up_last,
    down_last,
    up_first_other,
    down_first_other,
    up_last_other,
    down_last_other,
    block_out,
    two_grad,
    keep_hbm,
    send_hbm,
    norm_grads,
    first_in,
    second_in,
    out_grad,
    w_up,
    w_down,
    two_rows,
    pre_act,
    result,
    keep,
    send,
    in_sem,
    up_sem,
    down_sem,
    keep_sem,
    send_sem,
    out_sem,
):
    rows, features = first_in.shape
    items = rows // SEQ
    hidden_width = up_first.shape[3]
    piece_rows = up_first.shape[2]
    half = 2 * hidden_width
    up_parts = ((up_first, up_last), (up_first_other, up_last_other))
    down_parts = ((down_first, down_last), (down_first_other, down_last_other))

    def put(target, source, begin, width, semaphore):
        columns = pl.ds(begin, width)
        copy = pltpu.make_async_copy(source.at[:, columns], target.at[:, columns], semaphore)
        copy.start()
        return copy

    entries = [
        pltpu.make_async_copy(source, target, in_sem.at[index])
        for index, (source, target) in enumerate(
            ((first_hbm, first_in), (second_hbm, second_in), (out_grad_hbm, out_grad))
        )
    ]
    entries[0].start()
    entries[1].start()
    for first in range(2):

        @pl.when(place[0] == first)
        def _():
            for model in range(MODEL):
                side, y_rel = divmod(model, 2)
                for block in range(GROUPS):
                    source = up_parts[side][(block + first) % 2]
                    pltpu.make_async_copy(
                        source.at[y_rel, place[GROUPS + block]],
                        w_up.at[model, pl.ds(block * piece_rows, piece_rows), :],
                        up_sem.at[model],
                    ).start()
                for block in range(GROUPS):
                    source = down_parts[side][y_rel]
                    pltpu.make_async_copy(
                        source.at[(block + first) % 2, place[GROUPS + block]],
                        w_down.at[model, pl.ds(block * piece_rows, piece_rows), :],
                        down_sem.at[model],
                    ).start()

    entries[2].start()
    entries[0].wait()
    entries[1].wait()
    copies = []
    normed_one, _ = normalise(first_in[...])
    after_one = normed_one * norm[0:1, :] + norm[1:2, :]
    normed_two, _ = normalise(second_in[...])
    after_two = normed_two * norm[2:3, :] + norm[3:4, :]
    for item in range(items):
        begin = item * SEQ
        two_rows[begin : begin + QUERIES, :] = after_two[item * QUERIES : (item + 1) * QUERIES]
        two_rows[begin + QUERIES : begin + SEQ, :] = after_one[begin + QUERIES : begin + SEQ]
    feed_in = two_rows[...].astype(BF16)
    send[:, 2 * half : 2 * half + features] = feed_in
    copies.append(put(send_hbm, send, 2 * half, features, send_sem.at[4]))
    third_in = two_rows[...]
    for model in range(MODEL):
        side, y_rel = divmod(model, 2)
        target = (keep, send)[side]
        begin = y_rel * hidden_width
        pltpu.make_async_copy(w_up.at[model], w_up.at[model], up_sem.at[model]).wait()
        pre = dot_nn(feed_in, w_up[model])
        pre_act[:, model * hidden_width : (model + 1) * hidden_width] = pre
        act = (pre * gelu_cumulative(pre)).astype(BF16)
        target[:, begin : begin + hidden_width] = act
        semaphore = (keep_sem, send_sem)[side].at[y_rel]
        copies.append(put((keep_hbm, send_hbm)[side], target, begin, hidden_width, semaphore))
        pltpu.make_async_copy(w_down.at[model], w_down.at[model], down_sem.at[model]).wait()
        third_in = third_in + dot_nn(act, w_down[model])
    normed, inverse = normalise(third_in)
    result[...] = (normed * norm[4:5, :] + norm[5:6, :]).astype(BF16)
    copies.append(pltpu.make_async_copy(result, block_out, out_sem.at[0]))
    copies[-1].start()
    entries[2].wait()
    position = lax.broadcasted_iota(jnp.int32, (SEQ, features), 0)
    slope = jnp.concatenate(
        [
            jnp.where(
                position < lengths[item] + QUERIES,
                out_grad[item * SEQ : (item + 1) * SEQ, :].astype(F32),
                0.0,
            )
            for item in range(items)
        ],
        axis=0,
    )
    norm_grads[...] = jnp.zeros_like(norm_grads)
    norm_grads[4:5, :] = jnp.sum(slope * normed, axis=0, keepdims=True)
    norm_grads[5:6, :] = jnp.sum(slope, axis=0, keepdims=True)
    third_grad = norm_back(slope, normed, inverse, norm[4:5, :])
    grad_rows = third_grad.astype(BF16)
    send[:, 2 * half + features :] = grad_rows
    copies.append(put(send_hbm, send, 2 * half + features, features, send_sem.at[5]))
    total = third_grad
    for model in range(MODEL):
        side, y_rel = divmod(model, 2)
        target = (keep, send)[side]
        begin = half + y_rel * hidden_width
        pre = pre_act[:, model * hidden_width : (model + 1) * hidden_width]
        density = jnp.exp(-0.5 * pre * pre) * 0.3989422804014327
        slope_part = gelu_cumulative(pre) + pre * density
        grad_pre = (dot_nt(grad_rows, w_down[model]) * slope_part).astype(BF16)
        target[:, begin : begin + hidden_width] = grad_pre
        semaphore = (keep_sem, send_sem)[side].at[2 + y_rel]
        copies.append(put((keep_hbm, send_hbm)[side], target, begin, hidden_width, semaphore))
        total = total + dot_nt(grad_pre, w_up[model])
    two_rows[...] = total
    copies.append(pltpu.make_async_copy(two_rows, two_grad, out_sem.at[1]))
    copies[-1].start()
    for copy in copies:
        copy.wait()


def put_left(place, block, y_rel, keep, send, value):
    for along_x, target in ((0, keep), (1, send)):

        @pl.when(place[block] == along_x)
        def _(target=target):
            target[y_rel, place[GROUPS + block]] = value


def put_right(place, block, y_rel, keep, send, value):
    (keep, send)[y_rel][place[block], place[GROUPS + block]] = value


def feed_grad_kernel(
    place, hidden, rows, hidden_other, rows_other, left_keep, left_send, right_keep, right_send
):
    piece_rows = left_keep.shape[2]
    kind, y_step = pl.program_id(0), pl.program_id(1)

    @pl.when(kind == 0)
    def _():
        grad_up = dot_tn(rows[...], hidden[...])
        grad_up = (grad_up + dot_tn(rows_other[...], hidden_other[...])).astype(BF16)
        for block in range(GROUPS):
            span = slice(block * piece_rows, (block + 1) * piece_rows)
            put_left(place, block, y_step, left_keep, left_send, grad_up[span])

    for y_rel in range(2):

        @pl.when((kind == 1) & (y_step == y_rel))
        def _(y_rel=y_rel):
            grad_down = dot_tn(hidden[...], rows[...])
            grad_down = (grad_down + dot_tn(hidden_other[...], rows_other[...])).astype(BF16)
            for block in range(GROUPS):
                span = slice(block * piece_rows, (block + 1) * piece_rows)
                put_right(place, block, y_rel, right_keep, right_send, grad_down[span])


def cross_backward_kernel(
    two_grad,
    first_in,
    second_in,
    norm,
    w_cross,
    w_cross_out,
    queries,
    heads,
    key_values,
    norm_grads_in,
    keep,
    send,
    one_query_grad,
    norm_grads,
    head_grads,
    query_grads,
    grad_rows,
):
    features = first_in.shape[1]
    half = features // 2
    count = queries.shape[0]
    step = pl.program_id(0)
    items = pl.num_programs(0) - 3
    scale = HEAD ** (-0.5)

    @pl.when(step == 0)
    def _():
        two_query = query_rows(two_grad[...])
        normed, inverse = normalise(second_in[...])
        norm_grads[...] = norm_grads_in[...]
        norm_grads[2:3, :] = jnp.sum(two_query * normed, axis=0, keepdims=True)
        norm_grads[3:4, :] = jnp.sum(two_query, axis=0, keepdims=True)
        second_grad = norm_back(two_query, normed, inverse, norm[2:3, :])
        one_query_grad[...] = second_grad
        grad_rows[...] = second_grad.astype(BF16)
        head_grads[...] = dot_nt(grad_rows[...], w_cross_out[...]).astype(BF16)

    @pl.when(step < items)
    def _():
        head_mask = query_head_mask()
        span = pl.ds(pl.multiple_of(step * QUERIES, QUERIES), QUERIES)
        columns = [slice(begin, begin + WIDE) for begin in range(0, features, WIDE)]
        keys = [key_values[:, each] for each in columns]
        value_rows = [
            key_values[:, features + each.start : features + each.stop] for each in columns
        ]
        expanded = [head_rows(queries[span, each], head_mask) for each in columns]
        slopes = [head_rows(head_grads[span, each], head_mask) for each in columns]
        grad_probs = [dot_nt(*pair) for pair in zip(slopes, value_rows)]
        probs = patch_softmax(expanded, keys)
        inner = [
            jnp.sum(each * prob, axis=-1, keepdims=True) for each, prob in zip(grad_probs, probs)
        ]
        grad_scores = [
            (prob * (each - total)).astype(BF16)
            for prob, each, total in zip(probs, grad_probs, inner)
        ]
        grad_values = [
            dot_tn(prob.astype(BF16), slope).astype(BF16) for prob, slope in zip(probs, slopes)
        ]
        grad_keys = [
            (dot_tn(*pair) * scale).astype(BF16) for pair in zip(grad_scores, expanded)
        ]
        grad_queries = [dot_nn(*pair) for pair in zip(grad_scores, keys)]
        for index, each in enumerate(columns):
            query_grads[span, each] = (
                fold_heads(grad_queries[index], head_mask) * scale
            ).astype(BF16)
            for part in range(0, WIDE, WIDE // 2):
                side, place_at = divmod(each.start + part, half)
                target, lanes = (keep, send)[side], slice(part, part + WIDE // 2)
                target[:, place_at : place_at + WIDE // 2] = grad_keys[index][:, lanes]
                place_at += half
                target[:, place_at : place_at + WIDE // 2] = grad_values[index][:, lanes]

    @pl.when(step >= items)
    def _():
        for target in (keep, send):
            target[count:, :] = jnp.zeros((SLOT - count, features), BF16)

    @pl.when(step == items)
    def _():
        normed_one, _ = normalise(query_rows(first_in[...]))
        query_in = (normed_one * norm[0:1, :] + norm[1:2, :]).astype(BF16)
        for target in (keep, send):
            target[:count, :] = query_in

    @pl.when(step == items + 1)
    def _():
        for target in (keep, send):
            target[:count, :] = grad_rows[...]

    @pl.when(step == items + 2)
    def _():
        for side, target in enumerate((keep, send)):
            columns = slice(side * half, (side + 1) * half)
            target[:count, :half] = query_grads[:, columns]
            target[:count, half:] = heads[:, columns]
        one_query_grad[...] += dot_nt(query_grads[...], w_cross[...])


def image_grad_kernel(
    count,
    place,
    feats,
    keep_rows,
    other_rows,
    keep,
    other,
    left_keep,
    left_send,
    right_keep,
    right_send,
    total,
    spread,
):
    features = keep.shape[1]
    half = features // 2
    width = half // 2
    image_rows = feats.shape[2] // GROUPS
    image_half = image_rows // 2
    block_rows = features // GROUPS
    out_rows = width // GROUPS
    split = left_keep.shape[2]
    step, steps = pl.program_id(0), pl.num_programs(0)

    @pl.when(step == 0)
    def _():
        spread[...] = jnp.zeros_like(spread)

    for item in range(feats.shape[0]):
        spread[item * SLOT : item * SLOT + feats.shape[1], :] = feats[item]

    @pl.when(step == 0)
    def _():
        total[...] = dot_tn(spread[...], keep_rows[...])

    @pl.when((step > 0) & (step < steps // 2))
    def _():
        total[...] += dot_tn(spread[...], keep_rows[...])

    @pl.when(step >= steps // 2)
    def _():
        total[...] += dot_tn(spread[...], other_rows[...])

    @pl.when(step == steps - 1)
    def _():
        inputs, slopes = slice(0, count), slice(SLOT, SLOT + count)
        parts = slice(2 * SLOT, 2 * SLOT + count)
        grad_query = dot_tn(keep[inputs, :], keep[parts, :half]) + dot_tn(
            other[inputs, :], other[parts, :half]
        )
        grad_out = dot_tn(keep[parts, half:], keep[slopes, :]) + dot_tn(
            other[parts, half:], other[slopes, :]
        )
        for block in range(GROUPS):
            for y_rel in range(2):
                columns = slice(y_rel * width, (y_rel + 1) * width)
                image_part = [
                    total[
                        begin : begin + image_half,
                        kind + y_rel * width : kind + (y_rel + 1) * width,
                    ]
                    for begin in (block * image_rows, block * image_rows + image_half)
                    for kind in (0, half)
                ]
                begin = block * block_rows
                cross_part = [
                    grad_query[begin + part * out_rows : begin + (part + 1) * out_rows, columns]
                    for part in range(MODEL)
                ]
                begin = y_rel * width + block * out_rows
                piece = jnp.concatenate(
                    [
                        jnp.concatenate(image_part, axis=1),
                        jnp.concatenate(cross_part, axis=1),
                        grad_out[begin : begin + out_rows],
                    ],
                    axis=0,
                )
                put_left(place, block, y_rel, left_keep, left_send, piece[:split].astype(BF16))
                put_right(place, block, y_rel, right_keep, right_send, piece[split:].astype(BF16))


def self_backward_kernel(
    lengths,
    one_query_grad,
    two_grad,
    first_in,
    norm,
    hidden,
    qkv,
    heads,
    w_qkv,
    w_self_out,
    norm_grads_in,
    input_grad,
    keep,
    send,
    norm_total,
    one_grad,
    head_grads,
    grad_qkv,
):
    rows, features = hidden.shape
    items = rows // SEQ
    half = features // 2
    for item in range(items):
        begin = item * SEQ
        one_grad[begin : begin + QUERIES, :] = one_query_grad[
            item * QUERIES : (item + 1) * QUERIES, :
        ]
        one_grad[begin + QUERIES : begin + SEQ, :] = two_grad[begin + QUERIES : begin + SEQ, :]
    normed, inverse = normalise(first_in[...])
    gradient = one_grad[...]
    norm_sum = norm_grads_in[...] + jnp.concatenate(
        [
            jnp.sum(gradient * normed, axis=0, keepdims=True),
            jnp.sum(gradient, axis=0, keepdims=True),
            jnp.zeros((NORM_ROWS - 2, features), F32),
        ],
        axis=0,
    )
    norm_total[...] = norm_sum
    first_grad = norm_back(gradient, normed, inverse, norm[0:1, :])
    one_grad[...] = first_grad
    grad_rows = first_grad.astype(BF16)
    head_grads[...] = dot_nt(grad_rows, w_self_out[...]).astype(BF16)
    scale = HEAD ** (-0.5)
    for begin in range(0, rows, BLOCK):
        span = slice(begin, begin + BLOCK)
        mask = block_mask(lengths, begin // SEQ)
        for first in range(0, features // HEAD, HEADS_AT_ONCE):
            chosen = range(first, first + HEADS_AT_ONCE)
            queries, key_rows, value_rows = [
                [
                    qkv[span, kind * features + head * HEAD : kind * features + (head + 1) * HEAD]
                    for head in chosen
                ]
                for kind in range(3)
            ]
            slopes = [head_grads[span, head * HEAD : (head + 1) * HEAD] for head in chosen]
            scores = [dot_nt(*pair) for pair in zip(queries, key_rows)]
            grad_probs = [dot_nt(*pair) for pair in zip(slopes, value_rows)]
            probs = softmax([jnp.where(mask, each * scale, MASK_VALUE) for each in scores])
            inner = [
                jnp.sum(each * prob, axis=-1, keepdims=True)
                for each, prob in zip(grad_probs, probs)
            ]
            grad_scores = [
                (prob * (each - total)).astype(BF16)
                for prob, each, total in zip(probs, grad_probs, inner)
            ]
            results = (
                [dot_nn(*pair) * scale for pair in zip(grad_scores, key_rows)],
                [dot_tn(*pair) * scale for pair in zip(grad_scores, queries)],
                [dot_tn(prob.astype(BF16), slope) for prob, slope in zip(probs, slopes)],
            )
            for kind in range(3):
                begin_at = kind * features + first * HEAD
                grad_qkv[span, begin_at : begin_at + HEADS_AT_ONCE * HEAD] = jnp.concatenate(
                    [each.astype(BF16) for each in results[kind]], axis=1
                )
    total = one_grad[...]
    for kind in range(3):
        columns = slice(kind * features, (kind + 1) * features)
        total = total + dot_nt(grad_qkv[:, columns], w_qkv[:, columns])
        first = kind * features
        keep[:, kind * half : (kind + 1) * half] = grad_qkv[:, first : first + half]
        send[:rows, kind * half : (kind + 1) * half] = grad_qkv[:, first + half : first + features]
    input_grad[...] = total.astype(BF16)
    keep[:, 3 * half :] = heads[:, :half]
    send[:rows, 3 * half : 4 * half] = heads[:, half:]
    send[:rows, 4 * half : 6 * half] = hidden[...]
    send[:rows, 6 * half :] = grad_rows
    send[rows:, :] = jnp.zeros((send.shape[0] - rows, send.shape[1]), BF16)
    send[rows : rows + 16, :features] = jnp.concatenate(
        [norm_sum, jnp.zeros_like(norm_sum)], axis=0
    ).astype(BF16)


def self_grad_kernel(
    place, keep, send, other, norm_total, left_keep, left_send, right_keep, right_send
):
    features = norm_total.shape[1]
    rows = keep.shape[0]
    half = features // 2
    width = half // 2
    block_rows = features // GROUPS
    out_rows = width // GROUPS
    split = left_keep.shape[2]
    inputs, slopes = slice(4 * half, 6 * half), slice(6 * half, 8 * half)
    columns = slice(0, 3 * half)
    grad_in = dot_tn(send[:rows, inputs], keep[:, columns])
    grad_in = grad_in + dot_tn(other[:rows, inputs], other[:rows, columns])
    columns = slice(3 * half, 4 * half)
    grad_out = dot_tn(keep[:, columns], send[:rows, slopes])
    grad_out = grad_out + dot_tn(other[:rows, columns], other[:rows, slopes])
    norm_rows = norm_total[...] + other[rows : rows + 16, :features].astype(F32)[:NORM_ROWS]
    for block in range(GROUPS):
        span = slice(block * block_rows, (block + 1) * block_rows)
        for y_rel in range(2):
            pieces = [
                grad_in[span, kind * half + y_rel * width : kind * half + (y_rel + 1) * width]
                for kind in range(3)
            ]
            begin = y_rel * width + block * out_rows
            out_part = grad_out[begin : begin + out_rows]
            pieces.append(
                jnp.concatenate(
                    [out_part[:, part * width : (part + 1) * width] for part in range(MODEL)],
                    axis=0,
                )
            )
            piece = jnp.concatenate([jnp.concatenate(pieces, axis=1), norm_rows], axis=0)
            put_left(place, block, y_rel, left_keep, left_send, piece[:split].astype(BF16))
            put_right(place, block, y_rel, right_keep, right_send, piece[split:].astype(BF16))


def adam_step(weight, moment_one, moment_two, gradient, decay_rate):
    moment_one = BETA_ONE * moment_one + (1.0 - BETA_ONE) * gradient
    moment_two = BETA_TWO * moment_two + (1.0 - BETA_TWO) * gradient * gradient
    update = (
        moment_one
        / (1.0 - BETA_ONE**STEP)
        / (jnp.sqrt(moment_two / (1.0 - BETA_TWO**STEP)) + ADAM_EPSILON)
        + decay_rate * weight
    )
    return moment_one, moment_two, update


def place_sums(target, sums):
    column = lax.broadcasted_iota(jnp.int32, (1, LANES), 1)
    rows = []
    for kind in range(2):
        row = jnp.zeros((1, LANES), F32)
        for index, pair in sums.items():
            row = jnp.where(column == index, pair[kind], row)
        rows.append(row)
    target[...] = jnp.concatenate(rows, axis=0)


def sum_pair(weight, update):
    return jnp.sum(weight * weight), jnp.sum(update * update)


def feed_update_kernel(
    gradient,
    up,
    up_moments,
    down,
    down_moments,
    up_next,
    down_next,
    up_update,
    down_update,
    squares,
):
    rows = up.shape[0]
    sums = {}
    for index, weight, moments, following, result, span in (
        (8, up, up_moments, up_next, up_update, slice(0, rows)),
        (9, down, down_moments, down_next, down_update, slice(rows, None)),
    ):
        following[0], following[1], update = adam_step(
            weight[...], moments[0], moments[1], gradient[span, :], DECAY_RATE
        )
        result[...] = update
        sums[index] = sum_pair(weight[...], update)
    place_sums(squares, sums)


def image_update_kernel(gradient, weight, moments, following, result, squares):
    width = weight.shape[2]
    half = weight.shape[1] // 2
    sums = {}
    for kind in range(2):
        parts = []
        for part in range(2):
            span = slice(part * half, (part + 1) * half)
            lanes = slice((2 * part + kind) * width, (2 * part + kind + 1) * width)
            following[0, kind, span, :], following[1, kind, span, :], update = adam_step(
                weight[kind, span, :],
                moments[0, kind, span, :],
                moments[1, kind, span, :],
                gradient[:half, lanes],
                DECAY_RATE,
            )
            result[kind, span, :] = update
            parts.append(sum_pair(weight[kind, span, :], update))
        sums[6 + kind] = tuple(left + right for left, right in zip(*parts))
    place_sums(squares, sums)


def last_update_kernel(
    gradient,
    cross_gradient,
    norm_gradient,
    inward,
    inward_moments,
    outward,
    outward_moments,
    norm,
    norm_moments,
    inward_next,
    outward_next,
    norm_next,
    inward_update,
    outward_update,
    norm_update,
    squares,
):
    own_in, width = inward.shape[1:]
    own_out = outward.shape[1]
    cross_rows = cross_gradient.shape[0] - 2 * own_out
    cross_query = cross_gradient[cross_rows : cross_rows + own_out, :]
    gradients = [gradient[:own_in, kind * width : (kind + 1) * width] for kind in range(3)]
    gradients.append(
        jnp.concatenate(
            [cross_query[:, part * width : (part + 1) * width] for part in range(MODEL)], axis=0
        )
    )
    sums = {}
    for kind in range(4):
        inward_next[0, kind], inward_next[1, kind], update = adam_step(
            inward[kind],
            inward_moments[0, kind],
            inward_moments[1, kind],
            gradients[kind],
            DECAY_RATE,
        )
        inward_update[kind] = update
        sums[kind] = sum_pair(inward[kind], update)
    folded = gradient[:own_in, 3 * width :]
    self_out = jnp.concatenate(
        [folded[part * own_out : (part + 1) * own_out] for part in range(MODEL)], axis=1
    )
    for kind, part in enumerate((self_out, cross_gradient[cross_rows + own_out :, :])):
        outward_next[0, kind], outward_next[1, kind], update = adam_step(
            outward[kind], outward_moments[0, kind], outward_moments[1, kind], part, DECAY_RATE
        )
        outward_update[kind] = update
        sums[4 + kind] = sum_pair(outward[kind], update)
    norm_next[0], norm_next[1], update = adam_step(
        norm[...], norm_moments[0], norm_moments[1], norm_gradient[...], 0.0
    )
    norm_update[...] = update
    for kind in range(norm.shape[0]):
        sums[10 + kind] = sum_pair(norm[kind : kind + 1, :], update[kind : kind + 1, :])
    place_sums(squares, sums)


def apply_kernel(squares, *refs):
    groups = len(refs) // 5
    weights, averages, updates = refs[:groups], refs[groups : 2 * groups], refs[2 * groups : 3 * groups]
    new_weights, new_averages = refs[3 * groups : 4 * groups], refs[4 * groups : 5 * groups]
    trust_out, norms_out = refs[5 * groups :]
    sums = jnp.sum(squares[...], axis=0)
    trust = jnp.sqrt(sums[0:1]) * lax.rsqrt(sums[1:2] + SQUARE_EPSILON)
    trust_out[...] = trust
    norms_out[...] = jnp.sqrt(sums)
    column = lax.broadcasted_iota(jnp.int32, trust.shape, 1)

    def ratio(index):
        return jnp.sum(jnp.where(column == index, trust, 0.0), axis=1, keepdims=True)

    index = 0
    for weight, average, update, new_weight, new_average in zip(
        weights, averages, updates, new_weights, new_averages
    ):
        if len(weight.shape) == 3:
            spans = list(range(weight.shape[0]))
        elif weight.shape[0] == 6:
            spans = [slice(row, row + 1) for row in range(6)]
        else:
            spans = [slice(None)]
        for span in spans:
            value = weight[span] - LEARN_RATE * ratio(index) * update[span]
            new_weight[span] = value
            new_average[span] = AVERAGE_RATE * average[span] + (1.0 - AVERAGE_RATE) * value
            index += 1


SCALARS = pl.BlockSpec(memory_space=pltpu.SMEM)
WHOLE = pl.BlockSpec(memory_space=pltpu.VMEM)


def local_call(kernel, scalars, arrays, out_shapes, scratch, flops, name, limit):
    size = sum(a.size * a.dtype.itemsize for a in arrays)
    size += sum(a.size * a.dtype.itemsize for a in out_shapes)
    return pl.pallas_call(
        kernel,
        out_shape=tuple(out_shapes),
        in_specs=[SCALARS] * len(scalars) + [WHOLE] * len(arrays),
        out_specs=tuple([WHOLE] * len(out_shapes)),
        scratch_shapes=scratch,
        compiler_params=pltpu.CompilerParams(vmem_limit_bytes=limit * MIB),
        cost_estimate=pl.CostEstimate(flops=flops, bytes_accessed=size, transcendentals=0),
        name=name,
    )(*scalars, *arrays)


def shape_of(*dims, dtype=BF16):
    return jax.ShapeDtypeStruct(dims, dtype)


def part_shapes(left_rows, right_rows, features):
    left, right = shape_of(2, 4, left_rows, features), shape_of(2, 4, right_rows, features)
    return left, left, right, right


def like(array):
    return jax.ShapeDtypeStruct(array.shape, array.dtype)


def update_call(kernel, arrays, moments, weights, name):
    shapes = [like(each) for each in (*moments, *weights)] + [shape_of(2, LANES, dtype=F32)]
    return local_call(kernel, (), arrays, shapes, [], 0, name, 20)


def apply_call(squares, weights, averages, updates):
    shapes = [like(each) for each in (*weights, *averages)]
    shapes += [shape_of(1, LANES, dtype=F32), shape_of(2, LANES, dtype=F32)]
    return local_call(
        apply_kernel, (), (squares, *weights, *averages, *updates), shapes, [], 0, "apply", 60
    )


class Direct:
    def __init__(self, dp, mp):
        self.count = dp * mp
        self.mp = mp
        self.depth = dp // 2
        index = lax.axis_index("dp")
        block = jnp.arange(GROUPS, dtype=jnp.int32)
        along_x = (block % 2) ^ (index % 2)
        along_z = (index // 2 - block // 2) % self.depth
        self.place = jnp.concatenate([along_x, along_z]).astype(jnp.int32)

    def hop(self, values, flip):
        return lax.ppermute(values, AXES, [(i, i ^ flip) for i in range(self.count)])

    def hop_core(self, values):
        return self.hop(values, 1)

    def hop_y(self, values):
        return self.hop(values, 2)

    def hop_x(self, values):
        return self.hop(values, self.mp)

    def hop_z(self, values, distance):
        step = 2 * self.mp * distance
        return lax.ppermute(values, AXES, [(i, (i + step) % self.count) for i in range(self.count)])

    def spread_z(self, piece):
        return jnp.stack([piece] + [self.hop_z(piece, step) for step in range(1, self.depth)])


    def spread_first(self, held, split):
        return self.hop_y(held[:, :split]), self.hop_x(held[:, split:])

    def join_first(self, held, split, others):
        return jnp.stack([held[:, :split], others[0]]), jnp.stack([held[:, split:], others[1]])

    def spread_second(self, parts):
        return self.hop_x(parts[0]), self.hop_y(parts[1])

    def join_second(self, parts, others):
        left = jnp.stack([parts[0], others[0]])
        right = jnp.stack([parts[1], others[1]]).transpose(1, 0, 2, 3, 4)
        whole = jnp.concatenate([left, right], axis=3)
        return whole.reshape(SLOTS, *whole.shape[3:])


    def fold_first(self, grads):
        return self.hop_x(grads[1]), self.hop_y(grads[3])

    def fold_second(self, grads, others):
        return (
            self.hop_y(total([grads[0][1], others[0][1]])),
            self.hop_x(total([grads[2][1], others[1][1]])),
        )

    def kept(self, grads, others, last):
        return [[grads[2 * side][0], others[side][0], last[side]] for side in range(2)]

    def fold_z(self, sides):
        return [
            self.hop_z(total(*[[part[step] for part in parts] for parts in sides]), -step)
            for step in range(1, self.depth)
        ]

    def ring_z(self, sides, step, carried=None):
        addends = [[part[step] for part in parts] for parts in sides]
        own = total(*addends, dtype=F32)
        if carried is not None:
            own = own + carried.astype(F32)
        return self.hop_z(own.astype(BF16), 1)

    def finish(self, sides, others):
        own = total(*[[part[0] for part in parts] for parts in sides], dtype=F32)
        return total([own, *others], dtype=F32)


def total(*sides, dtype=BF16):
    sums = []
    for parts in sides:
        result = parts[0].astype(F32)
        for part in parts[1:]:
            result = result + part.astype(F32)
        sums.append(result.astype(dtype))
    return sums[0] if len(sums) == 1 else jnp.concatenate(sums, axis=0)


class Plain:
    def __init__(self, dp, mp):
        self.dp = dp
        self.mp = mp
        self.side = lax.axis_index("mp") // 2
        block = jnp.arange(GROUPS, dtype=jnp.int32)
        self.place = jnp.concatenate([block % 2, block // 2]).astype(jnp.int32)

    def hop_core(self, values):
        count = self.dp * self.mp
        return lax.ppermute(values, AXES, [(i, i ^ 2) for i in range(count)])

    def collect(self, piece):
        rows, width = piece.shape
        blocks = lax.all_gather(piece, AXES, axis=0).reshape(self.dp, self.mp, rows, width)
        rows = rows * self.dp // GROUPS
        blocks = blocks.transpose(1, 0, 2, 3).reshape(2, 2, 4, 2, rows, width)
        blocks = blocks.transpose(0, 3, 1, 2, 4, 5).reshape(2, SLOTS, rows, width)
        return jnp.where(self.side == 0, blocks, blocks[::-1])

    def joined(self, grads):
        left = jnp.stack(grads[:2])
        right = jnp.stack(grads[2:]).transpose(1, 0, 2, 3, 4)
        return jnp.concatenate([left, right], axis=3)

    def scatter(self, own):
        rows, width = own.shape[3:]
        own = own.transpose(1, 2, 0, 3, 4).reshape(1, 2, GROUPS, rows, width)
        both = jnp.zeros((2, *own.shape[1:]), F32)
        both = lax.dynamic_update_slice_in_dim(both, own.astype(F32), self.side, 0)
        both = both.reshape(self.mp, self.dp, rows * GROUPS // self.dp, width)
        both = both.transpose(1, 0, 2, 3).reshape(-1, width)
        return lax.psum_scatter(both, AXES, scatter_dimension=0, tiled=True)


def tie(*arrays):
    return lax.optimization_barrier(arrays)


def padded(feats):
    pad = ((0, 0), (0, SLOT - PATCHES), (0, 0))
    return jnp.pad(feats, pad).reshape(-1, feats.shape[2])


def tie(*arrays):
    return lax.optimization_barrier(arrays)


def add(left_side, right_side):
    return (left_side.astype(F32) + right_side.astype(F32)).astype(BF16)


def self_forward(place, lengths, hidden, begin):
    rows, features = hidden.shape
    return local_call(
        self_forward_kernel,
        (place, lengths),
        (hidden, *begin),
        (
            shape_of(rows, features, dtype=F32),
            shape_of(rows, 3 * features),
            shape_of(rows, features),
            shape_of(features, 3 * features),
            shape_of(features, features),
            shape_of(features, features),
            shape_of(features, features),
            shape_of(NORM_ROWS, features, dtype=F32),
        ),
        [pltpu.VMEM((features, features), F32), pltpu.VMEM((features, features), F32)],
        10 * rows * features * features,
        "self_forward",
        28,
    )


def fixed(shape):
    return pl.BlockSpec(shape, lambda *_: (0,) * len(shape))


def look(place, feats, image, first_in, norm, w_cross, w_cross_out):
    items, patches, encoded = feats.shape
    items = items // 2
    rows, features = items * SLOT, first_in.shape[1]
    count = items * QUERIES
    arrays = (*image, first_in, norm, w_cross, w_cross_out)
    return pl.pallas_call(
        look_kernel,
        out_shape=(
            shape_of(rows, 2 * features),
            shape_of(count, features, dtype=F32),
            shape_of(count, features),
            shape_of(count, features),
        ),
        grid_spec=pltpu.PrefetchScalarGridSpec(
            num_scalar_prefetch=1,
            grid=(items,),
            in_specs=[
                pl.BlockSpec(
                    (1, patches, encoded), lambda item, where: (where[2 * GROUPS] + item, 0, 0)
                )
            ]
            + [fixed(each.shape) for each in arrays],
            out_specs=(
                pl.BlockSpec((SLOT, 2 * features), lambda item, where: (item, 0)),
                fixed((count, features)),
                fixed((count, features)),
                fixed((count, features)),
            ),
            scratch_shapes=[
                pltpu.VMEM((encoded, 2 * features), BF16),
            ],
        ),
        compiler_params=pltpu.CompilerParams(vmem_limit_bytes=46 * MIB),
        cost_estimate=pl.CostEstimate(
            flops=5 * rows * encoded * features,
            bytes_accessed=2 * rows * (encoded + 2 * features) + 4 * encoded * features,
            transcendentals=0,
        ),
        name="look",
    )(place, feats, *arrays)


def feed(place, lengths, first_in, second_in, norm, out_grad, weights):
    rows, features = first_in.shape
    width = weights[0].shape[3]
    anywhere = pl.BlockSpec(memory_space=pl.ANY)
    return pl.pallas_call(
        feed_kernel,
        out_shape=(
            shape_of(rows, features),
            shape_of(rows, features, dtype=F32),
            shape_of(rows, 4 * width),
            shape_of(rows, 4 * width + 2 * features),
            shape_of(NORM_ROWS, features, dtype=F32),
        ),
        in_specs=[SCALARS, SCALARS, WHOLE] + [anywhere] * (3 + len(weights)),
        out_specs=(anywhere, anywhere, anywhere, anywhere, WHOLE),
        scratch_shapes=[
            pltpu.VMEM(first_in.shape, F32),
            pltpu.VMEM(second_in.shape, F32),
            pltpu.VMEM((rows, features), BF16),
            pltpu.VMEM((MODEL, features, width), BF16),
            pltpu.VMEM((MODEL, width, features), BF16),
            pltpu.VMEM((rows, features), F32),
            pltpu.VMEM((rows, MODEL * width), F32),
            pltpu.VMEM((rows, features), BF16),
            pltpu.VMEM((rows, 4 * width), BF16),
            pltpu.VMEM((rows, 4 * width + 2 * features), BF16),
            pltpu.SemaphoreType.DMA((3,)),
            pltpu.SemaphoreType.DMA((MODEL,)),
            pltpu.SemaphoreType.DMA((MODEL,)),
            pltpu.SemaphoreType.DMA((4,)),
            pltpu.SemaphoreType.DMA((6,)),
            pltpu.SemaphoreType.DMA((2,)),
        ],
        compiler_params=pltpu.CompilerParams(vmem_limit_bytes=58 * MIB),
        cost_estimate=pl.CostEstimate(
            flops=8 * rows * features * MODEL * width,
            bytes_accessed=4 * MODEL * width * features,
            transcendentals=0,
        ),
        name="feed",
    )(place, lengths, norm, first_in, second_in, out_grad, *weights)


def feed_grad(place, keep, send, other, rows):
    features = (send.shape[1] - keep.shape[1]) // 2
    width = keep.shape[1] // 4
    tokens = keep.shape[0]
    shapes = part_shapes(rows, rows, features)
    hidden_spec = pl.BlockSpec(
        (tokens, width), lambda kind, y_step, where: (0, 2 * (1 - kind) + y_step)
    )
    row_spec = pl.BlockSpec(
        (tokens, features), lambda kind, y_step, where: (0, 4 * width // features + kind)
    )
    return pl.pallas_call(
        feed_grad_kernel,
        out_shape=shapes,
        grid_spec=pltpu.PrefetchScalarGridSpec(
            num_scalar_prefetch=1,
            grid=(2, 2),
            in_specs=[hidden_spec, row_spec, hidden_spec, row_spec],
            out_specs=[fixed(shape.shape) for shape in shapes],
        ),
        compiler_params=pltpu.CompilerParams(vmem_limit_bytes=36 * MIB),
        cost_estimate=pl.CostEstimate(
            flops=4 * tokens * features * keep.shape[1],
            bytes_accessed=24 * tokens * features,
            transcendentals=0,
        ),
        name="feed_grad",
    )(place, keep, send, other, other)


def cross_backward(
    two_grad,
    first_in,
    second_in,
    norm,
    w_cross,
    w_cross_out,
    queries,
    heads,
    key_values,
    norm_grads,
):
    features = first_in.shape[1]
    count = queries.shape[0]
    items = key_values.shape[0] // SLOT
    rows = (items + 3) * SLOT
    arrays = (
        two_grad,
        first_in,
        second_in,
        norm,
        w_cross,
        w_cross_out,
        queries,
        heads,
        key_values,
        norm_grads,
    )
    specs = [fixed(each.shape) for each in arrays]
    specs[8] = pl.BlockSpec(
        (SLOT, 2 * features), lambda item: (jnp.minimum(item, items - 1), 0)
    )
    row_spec = pl.BlockSpec((SLOT, features), lambda item: (item, 0))
    return pl.pallas_call(
        cross_backward_kernel,
        grid=(items + 3,),
        out_shape=(
            shape_of(rows, features),
            shape_of(rows, features),
            shape_of(count, features, dtype=F32),
            shape_of(NORM_ROWS, features, dtype=F32),
        ),
        in_specs=specs,
        out_specs=(row_spec, row_spec, fixed((count, features)), fixed((NORM_ROWS, features))),
        scratch_shapes=[pltpu.VMEM((count, features), BF16)] * 3,
        compiler_params=pltpu.CompilerParams(vmem_limit_bytes=36 * MIB),
        cost_estimate=pl.CostEstimate(
            flops=20 * count * features * features,
            bytes_accessed=12 * rows * features,
            transcendentals=0,
        ),
        name="cross_backward",
    )(*arrays)


def image_grad(place, feats, keep, other):
    features = keep.shape[1]
    items, patches, encoded = feats.shape
    rows = items * SLOT
    piece = encoded // GROUPS // 2 + 2 * (features // MODEL // GROUPS)
    steps = 4
    block = rows // steps
    last = steps // 2 - 1
    shapes = part_shapes(IMAGE_SPLIT, piece - IMAGE_SPLIT, features)
    out_specs = [pl.BlockSpec(shape.shape, lambda step, where: (0, 0, 0, 0)) for shape in shapes]
    rest = pl.BlockSpec((4 * SLOT, features), lambda step, where: (items // 8, 0))
    return pl.pallas_call(
        functools.partial(image_grad_kernel, items // 2 * QUERIES),
        out_shape=shapes,
        grid_spec=pltpu.PrefetchScalarGridSpec(
            num_scalar_prefetch=1,
            grid=(steps,),
            in_specs=[
                pl.BlockSpec(
                    (items // steps, patches, encoded),
                    lambda step, where: (
                        (step + where[2 * GROUPS] // (items // steps)) % steps,
                        0,
                        0,
                    ),
                ),
                pl.BlockSpec((block, features), lambda step, where: (jnp.minimum(step, last), 0)),
                pl.BlockSpec(
                    (block, features), lambda step, where: (jnp.maximum(step - last - 1, 0), 0)
                ),
                rest,
                rest,
            ],
            out_specs=out_specs,
            scratch_shapes=[pltpu.VMEM((encoded, features), F32), pltpu.VMEM((block, encoded), BF16)],
        ),
        compiler_params=pltpu.CompilerParams(vmem_limit_bytes=34 * MIB),
        cost_estimate=pl.CostEstimate(
            flops=2 * rows * encoded * features,
            bytes_accessed=2 * rows * (encoded + features),
            transcendentals=0,
        ),
        name="image_grad",
    )(place, feats, keep, other, keep, other)


def self_backward(
    lengths,
    one_query_grad,
    two_grad,
    first_in,
    norm,
    hidden,
    qkv,
    heads,
    w_qkv,
    w_self_out,
    norm_grads,
):
    rows, features = hidden.shape
    return local_call(
        self_backward_kernel,
        (lengths,),
        (
            one_query_grad,
            two_grad,
            first_in,
            norm,
            hidden,
            qkv,
            heads,
            w_qkv,
            w_self_out,
            norm_grads,
        ),
        (
            shape_of(rows, features),
            shape_of(rows, 2 * features),
            shape_of(rows + 16, 4 * features),
            shape_of(NORM_ROWS, features, dtype=F32),
        ),
        [
            pltpu.VMEM((rows, features), F32),
            pltpu.VMEM((rows, features), BF16),
            pltpu.VMEM((rows, 3 * features), BF16),
        ],
        16 * rows * features * features,
        "self_backward",
        30,
    )


def self_grad(place, keep, send, other, norm_total):
    features = norm_total.shape[1]
    rows = features // GROUPS + NORM_ROWS
    return local_call(
        self_grad_kernel,
        (place,),
        (keep, send, other, norm_total),
        part_shapes(SELF_SPLIT, rows - SELF_SPLIT, features),
        [],
        8 * keep.shape[0] * features * features,
        "self_grad",
        24,
    )


def run_direct(hidden, feats, first_item, lengths, out_grad, image, begin, weights):
    moves = Direct(lax.axis_size("dp"), lax.axis_size("mp"))
    place = moves.place
    feats_place = jnp.concatenate([place, first_item[None].astype(jnp.int32)])
    begin_split = begin.shape[0] // 2
    image_split = image.shape[0] * 96 // 176
    feed_split = weights.shape[0] // 2

    begin = moves.spread_z(begin)
    begin, image, feats = tie(begin, image, feats)
    begin_others = moves.spread_first(begin, begin_split)
    image = moves.spread_z(image)
    begin_others, image, weights, feats = tie(begin_others, image, weights, feats)
    begin_parts = moves.join_first(begin, begin_split, begin_others)
    begin_others = moves.spread_second(begin_parts)
    image_others = moves.spread_first(image, image_split)
    weights = moves.spread_z(weights)
    begin_others, image_others, weights = tie(begin_others, image_others, weights)

    image_parts = moves.join_first(image, image_split, image_others)
    image_others = moves.spread_second(image_parts)
    weight_others = moves.spread_first(weights, feed_split)
    begin = moves.join_second(begin_parts, begin_others)
    begin_other = moves.hop_core(begin)
    first_in, qkv, heads, w_qkv, w_cross, w_self_out, w_cross_out, norm = self_forward(
        place, lengths, hidden, (begin, begin_other)
    )
    first_in, image_others, weight_others = tie(first_in, image_others, weight_others)
    image = moves.join_second(image_parts, image_others)
    weight_parts = moves.join_first(weights, feed_split, weight_others)
    image_other = moves.hop_core(image)
    weight_others = moves.spread_second(weight_parts)
    held_others = [moves.hop_core(part) for part in weight_parts]
    key_values, second_in, cross_queries, cross_heads = look(
        feats_place, feats, (image, image_other), first_in, norm, w_cross, w_cross_out
    )
    second_in, weight_others, held_others = tie(second_in, weight_others, held_others)
    last_others = [moves.hop_core(part) for part in weight_others]
    gathered = (*weight_parts, *weight_others, *held_others, *last_others)
    block_out, two_grad, feed_keep, feed_send, norm_grads = feed(
        place, lengths, first_in, second_in, norm, out_grad, gathered
    )

    feed_other = moves.hop_core(feed_send)
    cross_keep, cross_send, one_query_grad, norm_grads = cross_backward(
        two_grad,
        first_in,
        second_in,
        norm,
        w_cross,
        w_cross_out,
        cross_queries,
        cross_heads,
        key_values,
        norm_grads,
    )
    cross_send, feed_other = tie(cross_send, feed_other)
    cross_other = moves.hop_core(cross_send)
    feed_grads = feed_grad(place, feed_keep, feed_send, feed_other, feed_split)
    cross_other, feed_grads = tie(cross_other, feed_grads)
    feed_first = moves.fold_first(feed_grads)
    image_grads = image_grad(feats_place, feats, cross_keep, cross_other)
    one_query_grad, image_grads, feed_first = tie(one_query_grad, image_grads, feed_first)
    feed_second = moves.fold_second(feed_grads, feed_first)
    image_first = moves.fold_first(image_grads)
    input_grad, self_keep, self_send, norm_total = self_backward(
        lengths,
        one_query_grad,
        two_grad,
        first_in,
        norm,
        hidden,
        qkv,
        heads,
        w_qkv,
        w_self_out,
        norm_grads,
    )
    self_send, image_first, feed_second = tie(self_send, image_first, feed_second)
    self_other = moves.hop_core(self_send)
    feed_kept = moves.kept(feed_grads, feed_first, feed_second)
    feed_other = moves.ring_z(feed_kept, 1)
    image_second = moves.fold_second(image_grads, image_first)
    self_grads = self_grad(place, self_keep, self_send, self_other, norm_total)
    self_grads, feed_other = tie(self_grads, feed_other)
    self_first = moves.fold_first(self_grads)
    feed_other = moves.ring_z(feed_kept, 2, feed_other)
    feed_other, image_second = tie(feed_other, image_second)
    image_kept = moves.kept(image_grads, image_first, image_second)
    feed_other = moves.ring_z(feed_kept, 3, feed_other)
    image_other = moves.ring_z(image_kept, 1)
    self_first, image_other, feed_other = tie(self_first, image_other, feed_other)
    self_second = moves.fold_second(self_grads, self_first)
    image_other = moves.ring_z(image_kept, 2, image_other)
    feed_sum = moves.finish(feed_kept, [feed_other])
    image_other, self_second = tie(image_other, self_second)
    image_other = moves.ring_z(image_kept, 3, image_other)
    self_kept = moves.kept(self_grads, self_first, self_second)
    self_others = moves.fold_z(self_kept)
    image_sum = moves.finish(image_kept, [image_other])
    in_sum = moves.finish(self_kept, self_others)
    return block_out, input_grad, in_sum, image_sum, feed_sum


def run_plain(hidden, feats, first_item, lengths, out_grad, image, begin, weights):
    moves = Plain(lax.axis_size("dp"), lax.axis_size("mp"))
    place = moves.place
    feats_place = jnp.concatenate([place, first_item[None].astype(jnp.int32)])
    features = hidden.shape[1]
    width = features // MODEL
    block_rows, out_rows = features // GROUPS, width // GROUPS
    own_in, own_out = block_rows * GROUPS // moves.dp, out_rows * GROUPS // moves.dp
    half = block_rows // 2
    part = begin.shape[0] - NORM_ROWS
    inward = moves.collect(begin[:own_in])
    cross_out = moves.collect(begin[own_in : own_in + own_out])
    self_out = moves.collect(begin[own_in + own_out : part])
    norm_all = lax.psum(begin[part:].astype(F32), AXES).astype(BF16)
    norm_first = jnp.zeros((2, SLOTS, NORM_ROWS, features), BF16).at[0, 0].set(norm_all)
    begin = jnp.concatenate(
        [
            inward[:, :, :half],
            cross_out,
            jnp.zeros_like(norm_first),
            inward[:, :, half:],
            self_out,
            norm_first,
        ],
        axis=2,
    )
    image = moves.collect(image)
    own_up = weights.shape[0] // 2
    ups, downs = [
        moves.collect(part).reshape(2, 2, 2, 4, -1, features)
        for part in (weights[:own_up], weights[own_up:])
    ]
    gathered = tuple(
        part
        for side in range(2)
        for last in range(2)
        for part in (ups[side, last], downs[side, :, last])
    )
    first_in, qkv, heads, w_qkv, w_cross, w_self_out, w_cross_out, norm = self_forward(
        place, lengths, hidden, (begin[0], begin[1])
    )
    key_values, second_in, cross_queries, cross_heads = look(
        feats_place, feats, (image[0], image[1]), first_in, norm, w_cross, w_cross_out
    )
    block_out, two_grad, feed_keep, feed_send, norm_grads = feed(
        place, lengths, first_in, second_in, norm, out_grad, gathered
    )
    feed_half = gathered[0].shape[2]
    feed_grads = feed_grad(place, feed_keep, feed_send, moves.hop_core(feed_send), feed_half)
    cross_keep, cross_send, one_query_grad, norm_grads = cross_backward(
        two_grad,
        first_in,
        second_in,
        norm,
        w_cross,
        w_cross_out,
        cross_queries,
        cross_heads,
        key_values,
        norm_grads,
    )
    image_grads = image_grad(feats_place, feats, cross_keep, moves.hop_core(cross_send))
    input_grad, self_keep, self_send, norm_total = self_backward(
        lengths,
        one_query_grad,
        two_grad,
        first_in,
        norm,
        hidden,
        qkv,
        heads,
        w_qkv,
        w_self_out,
        norm_grads,
    )
    self_grads = self_grad(place, self_keep, self_send, moves.hop_core(self_send), norm_total)

    def beside(values):
        count = values.shape[-2] // MODEL
        return jnp.concatenate(
            [values[..., part * count : (part + 1) * count, :] for part in range(MODEL)], axis=-1
        )

    def below(values):
        count = values.shape[-1] // MODEL
        return jnp.concatenate(
            [values[..., part * count : (part + 1) * count] for part in range(MODEL)], axis=-2
        )

    grads = moves.joined(self_grads)
    in_part = moves.scatter(grads[..., :block_rows, : 3 * width])
    self_out = moves.scatter(beside(grads[..., :block_rows, 3 * width :]))
    norm_sum = lax.psum(norm_total, AXES)
    in_sum = jnp.concatenate([jnp.concatenate([in_part, below(self_out)], axis=1), norm_sum])
    grads = moves.joined(image_grads)
    image_rows = grads.shape[3] - 2 * out_rows
    image_part = grads[..., :image_rows, :]
    image_part = jnp.concatenate(
        [image_part[..., : features // 2], image_part[..., features // 2 :]], axis=3
    )
    image_part = moves.scatter(image_part)
    image_half = image_part.shape[0] // 2
    image_part = jnp.concatenate([image_part[:image_half], image_part[image_half:]], axis=1)
    cross_query = moves.scatter(below(grads[..., image_rows : image_rows + out_rows, :]))
    cross_out = moves.scatter(grads[..., image_rows + out_rows :, :])
    image_sum = jnp.concatenate([image_part, beside(cross_query), cross_out])
    grads = moves.joined(feed_grads)
    feed_sum = jnp.concatenate(
        [moves.scatter(jnp.stack(feed_grads[:2])), moves.scatter(grads[..., feed_half:, :])]
    )
    return block_out, input_grad, in_sum, image_sum, feed_sum


def per_device(
    hidden_in,
    image_feats,
    caption_lengths,
    out_grad,
    proj_in,
    proj_in_moments,
    proj_in_average,
    proj_out,
    proj_out_moments,
    proj_out_average,
    image_kv,
    image_kv_moments,
    image_kv_average,
    feed_up,
    feed_up_moments,
    feed_up_average,
    feed_down,
    feed_down_moments,
    feed_down_average,
    norm_params,
    norm_params_moments,
    norm_params_average,
):
    data_ways, model_ways = lax.axis_size("dp"), lax.axis_size("mp")
    data_index, model_index = lax.axis_index("dp"), lax.axis_index("mp")
    rows, features = hidden_in.shape
    items = rows // SEQ
    width = features // model_ways
    own_norm = norm_params.shape[1]
    norm_begin = (model_index * data_ways + data_index) * own_norm
    lengths = lax.dynamic_slice_in_dim(caption_lengths, model_index * items, items, 0)
    direct = data_ways == GROUPS and model_ways == MODEL
    if direct:
        feats = lax.dynamic_slice_in_dim(image_feats, model_index // 2 * 2 * items, 2 * items, 0)
        first_item = model_index % 2 * items
    else:
        feats = jnp.concatenate(
            [
                lax.dynamic_slice_in_dim(image_feats, (model_index % 2 + 2 * side) * items, items, 0)
                for side in range(2)
            ]
        )
        first_item = model_index // 2 * items
    image_piece = jnp.concatenate([image_kv[0], image_kv[1]], axis=1).astype(BF16)
    in_piece = jnp.concatenate([proj_in[kind] for kind in range(4)], axis=1).astype(BF16)
    out_pieces = [proj_out[kind].astype(BF16) for kind in range(2)]
    feed_piece = jnp.concatenate([feed_up, feed_down], axis=0).astype(BF16)
    norm_rows = lax.dynamic_update_slice(
        jnp.zeros((NORM_ROWS, features), F32), norm_params, (0, norm_begin)
    ).astype(BF16)
    own_in, own_out, own_image = proj_in.shape[1], proj_out.shape[1], image_kv.shape[1]
    if direct:
        run, half = run_direct, own_in // 2
        begin_piece = jnp.concatenate(
            [
                in_piece[:half],
                out_pieces[1],
                jnp.zeros_like(norm_rows),
                in_piece[half:],
                out_pieces[0],
                norm_rows,
            ],
            axis=0,
        )
    else:
        run = run_plain
        begin_piece = jnp.concatenate(
            [in_piece, out_pieces[1], out_pieces[0], norm_rows], axis=0
        )
    block_out, input_grad, in_sum, image_sum, feed_sum = run(
        hidden_in, feats, first_item, lengths, out_grad, image_piece, begin_piece, feed_piece
    )
    norm_shard = lax.dynamic_slice(in_sum[own_in:], (0, norm_begin), norm_params.shape)
    up_next, down_next, up_update, down_update, feed_squares = update_call(
        feed_update_kernel,
        (feed_sum, feed_up, feed_up_moments, feed_down, feed_down_moments),
        (feed_up_moments, feed_down_moments),
        (feed_up, feed_down),
        "feed_update",
    )
    image_next, image_update, image_squares = update_call(
        image_update_kernel,
        (image_sum, image_kv, image_kv_moments),
        (image_kv_moments,),
        (image_kv,),
        "image_update",
    )
    in_next, out_next, norm_next, in_update, out_update, norm_update, last_squares = update_call(
        last_update_kernel,
        (
            in_sum,
            image_sum,
            norm_shard,
            proj_in,
            proj_in_moments,
            proj_out,
            proj_out_moments,
            norm_params,
            norm_params_moments,
        ),
        (proj_in_moments, proj_out_moments, norm_params_moments),
        (proj_in, proj_out, norm_params),
        "last_update",
    )
    own_squares = feed_squares + image_squares + last_squares
    ways = data_ways * model_ways
    copies = jnp.broadcast_to(own_squares[None], (ways,) + own_squares.shape)
    squares = lax.all_to_all(copies, AXES, 0, 0, tiled=True)
    results = apply_call(
        squares,
        (proj_in, proj_out, image_kv, feed_up, feed_down, norm_params),
        (
            proj_in_average,
            proj_out_average,
            image_kv_average,
            feed_up_average,
            feed_down_average,
            norm_params_average,
        ),
        (in_update, out_update, image_update, up_update, down_update, norm_update),
    )
    new_weights, new_averages, (trust, norms) = results[:6], results[6:12], results[12:]
    moments = (in_next, out_next, image_next, up_next, down_next, norm_next)
    outputs = [
        each for group in zip(new_weights, moments, new_averages) for each in group
    ]
    tensors = sum(each.shape[0] for each in (proj_in, proj_out, image_kv, norm_params)) + 2
    return (block_out, input_grad, *outputs, trust[0, :tensors], norms[:, :tensors])


def solution(mesh):
    rows = P(AXES, None)
    by_column = P(None, "dp", "mp")
    by_row = P(None, ("mp", "dp"), None)
    weights = (
        by_column,
        P(None, None, "dp", "mp"),
        by_column,
        by_row,
        P(None, None, ("mp", "dp"), None),
        by_row,
        by_column,
        P(None, None, "dp", "mp"),
        by_column,
        P("dp", "mp"),
        P(None, "dp", "mp"),
        P("dp", "mp"),
        P(("mp", "dp"), None),
        P(None, ("mp", "dp"), None),
        P(("mp", "dp"), None),
        P(None, ("mp", "dp")),
        P(None, None, ("mp", "dp")),
        P(None, ("mp", "dp")),
    )
    return jax.shard_map(
        per_device,
        mesh=mesh,
        in_specs=(rows, P("dp", None, None), P("dp"), rows, *weights),
        out_specs=(rows, rows, *weights, P(), P()),
        check_vma=False,
    )
```

profile of v0, /device:TPU:0, one launch (start us, length us, event | category | flops | bytes accessed | tf_op | source)
XLA Modules:
  0.0 353.4 jit_solution(8656178818172176830)
XLA Ops:
  2.4 3.3 collective-permute-start
  5.7 2.6 collective-permute-start.1
  9.6 5.9 %constant_dynamic-slice_fusion.1 = bf16[16,257,1408]{2,0,1:T(8,128)(2,1)S(1)} fusion(bf16[32,257,1408]{2,0,1:T(8,128)(2,1)} %param.23, s32[]{:T(128)S(6)} %select_n.51), kind=kLoop, calls=%fused_computation.109 | loop fusion | bytes 23158788 | tf_op jit(solution)/shard_map/dynamic_slice | solution.py:1693
  15.5 7.8 %copy.50.feats = bf16[16,257,1408]{2,1,0:T(8,128)(2,1)} copy(bf16[16,257,1408]{2,0,1:T(8,128)(2,1)S(1)} %constant_dynamic-slice_fusion.1) | data formatting | bytes 23158784 | tf_op jit(solution)/shard_map/optimization_barrier | solution.py:1130
  24.6 1.5 collective-permute-start.3
  27.7 5.7 %collective-permute-start.5 = (bf16[176,384]{1,0:T(8,128)(2,1)S(1)}, bf16[176,384]{1,0:T(8,128)(2,1)S(1)}, u32[]{:S(2)}, u32[]{:S(2)}) collective-permute-start(bf16[176,384]{1,0:T(8,128)(2,1)S(1)} %pad_maximum_fusion.18), channel_id=1, source_target_pairs={{0,8},{1,9},{2,10},{3,11},{4,12},{5,13},{6,14},{7,15},{8,16},{9,17... | collective-permute-start | bytes 405512 | tf_op jit(solution)/shard_map/ppermute | solution.py:1023
  33.4 1.6 collective-permute-start.6
  35.8 3.1 collective-permute-done.5
  38.9 4.2 %collective-permute-done.6 = bf16[176,384]{1,0:T(8,128)(2,1)S(1)} collective-permute-done((bf16[176,384]{1,0:T(8,128)(2,1)S(1)}, bf16[176,384]{1,0:T(8,128)(2,1)S(1)}, u32[]{:S(2)}, u32[]{:S(2)}) %collective-permute-start.6) | collective-permute-done | bytes 135200 | tf_op jit(solution)/shard_map/ppermute | solution.py:1023
  44.7 3.4 collective-permute-start.12
  48.1 1.7 collective-permute-start.13
  51.2 6.1 %collective-permute-done.12 = bf16[192,768]{1,0:T(8,128)(2,1)S(1)} collective-permute-done((bf16[192,768]{1,0:T(8,128)(2,1)S(1)}, bf16[192,768]{1,0:T(8,128)(2,1)S(1)}, u32[]{:S(2)}, u32[]{:S(2)}) %collective-permute-start.12) | collective-permute-done | bytes 294944 | tf_op jit(solution)/shard_map/ppermute | solution.py:1023
  58.8 8.7 %collective-permute-done.13 = bf16[192,768]{1,0:T(8,128)(2,1)S(1)} collective-permute-done((bf16[192,768]{1,0:T(8,128)(2,1)S(1)}, bf16[192,768]{1,0:T(8,128)(2,1)S(1)}, u32[]{:S(2)}, u32[]{:S(2)}) %collective-permute-start.13) | collective-permute-done | bytes 294944 | tf_op jit(solution)/shard_map/ppermute | solution.py:1023
  70.2 5.1 %collective-permute-done.11 = bf16[4,80,384]{2,1,0:T(8,128)(2,1)S(1)} collective-permute-done((bf16[4,80,384]{2,1,0:T(8,128)(2,1)S(1)}, bf16[4,80,384]{2,1,0:T(8,128)(2,1)S(1)}, u32[]{:S(2)}, u32[]{:S(2)}) %collective-permute-start.11) | collective-permute-done | bytes 245792 | tf_op jit(solution)/shard_map/ppermute | solution.py:1010
  76.9 2.2 copy.46
  80.3 1.6 collective-permute-start.16
  86.2 12.2 %self_forward.1 = (f32[512,768]{1,0:T(8,128)S(1)}, bf16[512,2304]{1,0:T(8,128)(2,1)S(1)}, bf16[512,768]{1,0:T(8,128)(2,1)S(1)}, bf16[768,2304]{1,0:T(8,128)(2,1)...) custom-call(s32[16]{0:T(128)S(1)} %pad_add_fusion.place, ...), custom_call_target="tpu_custom_call" | custom-call | flops 3019898880 | bytes 20471808 | tf_op jit(solution)/shard_map/self_forward/pallas_call | solution.py:960
  98.4 1.7 copy-done.47
  103.4 5.5 %collective-permute-done.17 = bf16[2,4,80,384]{3,2,1,0:T(8,128)(2,1)S(1)} collective-permute-done((bf16[2,4,80,384]{3,2,1,0:T(8,128)(2,1)S(1)}, bf16[2,4,80,384]{3,2,1,0:T(8,128)(2,1)S(1)}, u32[]{:S(2)}, u32[]{:S(2)}) %collective-permute-start.17) | collective-permute-done | bytes 491552 | tf_op jit(solution)/shard_map/ppermute | solution.py:1010
  111.7 1.5 collective-permute-start.22
  116.0 21.3 %look.1 = (bf16[2176,1536]{1,0:T(8,128)(2,1)}, f32[256,768]{1,0:T(8,128)S(1)}, bf16[256,768]{1,0:T(8,128)(2,1)S(1)}, bf16[256,768]{1,0:T(8,128)(2,1)S(1)}) custom-call(s32[17]{0:T(128)S(1)} %pad_add_fusion.1.place, bf16[16,257,1408]{2,1,0:T(8,128)(2,1)} %copy.50.feats, bf16[16,176,384]{2,1,0:T(8,128)(2,1)S(1)} %bitcast.209, ...), custom_call_target="tpu_custom_call" | custom-call | flops 11765022720 | bytes 17137664 | tf_op jit(solution)/shard_map/look/pallas_call | solution.py:1170
  140.1 2.8 collective-permute-done.21.up_last
  143.5 3.1 collective-permute-done.25.up_last_other
  147.7 19.2 %feed.1 = (bf16[512,768]{1,0:T(8,128)(2,1)}, f32[512,768]{1,0:T(8,128)}, bf16[512,3072]{1,0:T(8,128)(2,1)}, bf16[512,4608]{1,0:T(8,128)(2,1)}, f32[8,768]{1,0:T(8,128)}) custom-call(s32[16]{0:T(128)} %copy-done.42, s32[8]{0:T(128)} %copy-done.44, f32[8,768]{1,0:T(8,128)} %copy-done.33, f32[512,768]{1,0:T(8,128)} %copy-done.4, f32[256,768]{1,0:T(8,128)} %copy-done.17, ...), custom_call_target="tpu_custom_call" | custom-call | flops 9663676416 | bytes 9437184 | tf_op jit(solution)/shard_map/feed/pallas_call | solution.py:1211
  171.2 15.6 %cross_backward.1 = (bf16[2992,768]{1,0:T(8,128)(2,1)S(1)}, bf16[2992,768]{1,0:T(8,128)(2,1)}, f32[256,768]{1,0:T(8,128)S(1)}, f32[8,768]{1,0:T(8,128)S(1)}) custom-call(f32[512,768]{1,0:T(8,128)S(1)} %copy-done.7, f32[512,768]{1,0:T(8,128)S(1)} %copy-done.6, f32[256,768]{1,0:T(8,128)S(1)} %copy-done.18, f32[8,768]{1,0:T(8,128)S(1)} %copy-done.34, ...), custom_call_target="tpu_custom_call" | custom-call | flops 3019898880 | bytes 27574272 | tf_op jit(solution)/shard_map/cross_backward/pallas_call | solution.py:1313
  186.8 2.2 copy-done.38
  189.4 1.9 copy-done.46
  191.2 8.5 %feed_grad.1 = (bf16[2,4,96,768]{3,2,1,0:T(8,128)(2,1)S(1)}, bf16[2,4,96,768]{3,2,1,0:T(8,128)(2,1)S(1)}, bf16[2,4,96,768]{3,2,1,0:T(8,128)(2,1)S(1)}, bf16[2,4,96,768]{3,2,1,0:T(8,128)(2,1)S(1)}) custom-call(s32[16]{0:T(128)S(1)} %copy-done.43, bf16[512,3072]{1,0:T(8,128)(2,1)S(1)} %copy-done.46, bf16[512,4608]{1,0:T(8,128)(2,1)S(1)} %copy-done.37, ...), custom_call_target="tpu_custom_call" | custom-call | flops 4831838208 | bytes 9437184 | tf_op jit(solution)/shard_map/feed_grad/pallas_call | solution.py:1261
  201.8 2.3 copy-done.39
  204.1 19.1 %image_grad.1 = (bf16[2,4,64,768]{3,2,1,0:T(8,128)(2,1)S(1)}, bf16[2,4,64,768]{3,2,1,0:T(8,128)(2,1)S(1)}, bf16[2,4,72,768]{3,2,1,0:T(8,128)(2,1)S(1)}, bf16[2,4,72,768]{3,2,1,0:T(8,128)(2,1)S(1)}) custom-call(s32[17]{0:T(128)S(1)} %pad_add_fusion.1.place, bf16[16,257,1408]{2,1,0:T(8,128)(2,1)} %copy.50.feats, bf16[2992,768]{1,0:T(8,128)(2,1)S(1)} %copy-done.39, ...), custom_call_target="tpu_custom_call" | custom-call | flops 9412018176 | bytes 18939904 | tf_op jit(solution)/shard_map/image_grad/pallas_call | solution.py:1346
  223.3 4.6 %collective-permute-done.29 = bf16[2,4,96,768]{3,2,1,0:T(8,128)(2,1)S(1)} collective-permute-done((bf16[2,4,96,768]{3,2,1,0:T(8,128)(2,1)S(1)}, bf16[2,4,96,768]{3,2,1,0:T(8,128)(2,1)S(1)}, u32[]{:S(2)}, u32[]{:S(2)}) %collective-permute-start.29) | collective-permute-done | bytes 1179680 | tf_op jit(solution)/shard_map/ppermute | solution.py:1010
  233.4 1.7 copy-done.50
  235.1 15.7 %self_backward.1 = (bf16[512,768]{1,0:T(8,128)(2,1)}, bf16[512,1536]{1,0:T(8,128)(2,1)S(1)}, bf16[528,3072]{1,0:T(8,128)(2,1)S(1)}, f32[8,768]{1,0:T(8,128)S(1)}) custom-call(s32[8]{0:T(128)S(1)} %copy-done.45, f32[256,768]{1,0:T(8,128)S(1)} %get-tuple-element.197.one_query_grad, f32[512,768]{1,0:T(8,128)S(1)} %copy-done.8, f32[512,768]{1,0:T(8,128)S(1)} %copy-done.6, ...), custom_call_target="tpu_custom_call" | custom-call | flops 4831838208 | bytes 18259968 | tf_op jit(solution)/shard_map/self_backward/pallas_call | solution.py:960
  250.8 11.2 %collective-permute-done.33 = bf16[4,96,768]{2,1,0:T(8,128)(2,1)S(1)} collective-permute-done((bf16[4,96,768]{2,1,0:T(8,128)(2,1)S(1)}, bf16[4,96,768]{2,1,0:T(8,128)(2,1)S(1)}, u32[]{:S(2)}, u32[]{:S(2)}) %collective-permute-start.33) | collective-permute-done | bytes 589856 | tf_op jit(solution)/shard_map/ppermute | solution.py:1010
  264.0 4.6 %collective-permute-start.36 = (bf16[192,768]{1,0:T(8,128)(2,1)S(1)}, bf16[192,768]{1,0:T(8,128)(2,1)S(1)}, u32[]{:S(2)}, u32[]{:S(2)}) collective-permute-start(bf16[192,768]{1,0:T(8,128)(2,1)S(1)} %pad_maximum_fusion.12), channel_id=1, source_target_pairs={{0,8},{1,9},{2,10},{3,11},{4,12},{5,13},{6,14},{7,15},{8,16},{9,17... | collective-permute-start | bytes 884744 | tf_op jit(solution)/shard_map/ppermute | solution.py:1023
  269.5 5.9 %self_grad.1 = (bf16[2,4,48,768]{3,2,1,0:T(8,128)(2,1)S(1)}, bf16[2,4,48,768]{3,2,1,0:T(8,128)(2,1)S(1)}, bf16[2,4,56,768]{3,2,1,0:T(8,128)(2,1)S(1)}, bf16[2,4,56,768]{3,2,1,0:T(8,128)(2,1)S(1)}) custom-call(s32[16]{0:T(128)S(1)} %copy-done.43, bf16[512,1536]{1,0:T(8,128)(2,1)S(1)} %get-tuple-element.213.keep, ...), custom_call_target="tpu_custom_call" | custom-call | flops 2415919104 | bytes 10641408 | tf_op jit(solution)/shard_map/self_grad/pallas_call | solution.py:960
  275.4 3.7 %collective-permute-done.36 = bf16[192,768]{1,0:T(8,128)(2,1)S(1)} collective-permute-done((bf16[192,768]{1,0:T(8,128)(2,1)S(1)}, bf16[192,768]{1,0:T(8,128)(2,1)S(1)}, u32[]{:S(2)}, u32[]{:S(2)}) %collective-permute-start.36) | collective-permute-done | bytes 294944 | tf_op jit(solution)/shard_map/ppermute | solution.py:1023
  280.9 9.0 %collective-permute-done.39 = bf16[192,768]{1,0:T(8,128)(2,1)S(1)} collective-permute-done((bf16[192,768]{1,0:T(8,128)(2,1)S(1)}, bf16[192,768]{1,0:T(8,128)(2,1)S(1)}, u32[]{:S(2)}, u32[]{:S(2)}) %collective-permute-start.39) | collective-permute-done | bytes 294944 | tf_op jit(solution)/shard_map/ppermute | solution.py:1023
  290.8 13.4 %collective-permute-done.42 = bf16[136,768]{1,0:T(8,128)(2,1)S(1)} collective-permute-done((bf16[136,768]{1,0:T(8,128)(2,1)S(1)}, bf16[136,768]{1,0:T(8,128)(2,1)S(1)}, u32[]{:S(2)}, u32[]{:S(2)}) %collective-permute-start.42) | collective-permute-done | bytes 208928 | tf_op jit(solution)/shard_map/ppermute | solution.py:1023
  305.9 1.7 feed_update.1
  307.6 7.2 %collective-permute-done.44 = bf16[136,768]{1,0:T(8,128)(2,1)S(1)} collective-permute-done((bf16[136,768]{1,0:T(8,128)(2,1)S(1)}, bf16[136,768]{1,0:T(8,128)(2,1)S(1)}, u32[]{:S(2)}, u32[]{:S(2)}) %collective-permute-start.44) | collective-permute-done | bytes 208928 | tf_op jit(solution)/shard_map/ppermute | solution.py:1023
  315.3 2.1 collective-permute-start.50
  317.4 1.5 collective-permute-start.47
  318.9 4.8 %collective-permute-done.48 = bf16[104,768]{1,0:T(8,128)(2,1)S(1)} collective-permute-done((bf16[104,768]{1,0:T(8,128)(2,1)S(1)}, bf16[104,768]{1,0:T(8,128)(2,1)S(1)}, u32[]{:S(2)}, u32[]{:S(2)}) %collective-permute-start.48) | collective-permute-done | bytes 159776 | tf_op jit(solution)/shard_map/ppermute | solution.py:1023
  323.7 7.8 %collective-permute-done.49 = bf16[104,768]{1,0:T(8,128)(2,1)S(1)} collective-permute-done((bf16[104,768]{1,0:T(8,128)(2,1)S(1)}, bf16[104,768]{1,0:T(8,128)(2,1)S(1)}, u32[]{:S(2)}, u32[]{:S(2)}) %collective-permute-start.49) | collective-permute-done | bytes 159776 | tf_op jit(solution)/shard_map/ppermute | solution.py:1023
  337.3 2.6 all-to-all-start
  340.5 6.7 %all-to-all-done.squares = f32[32,2,128]{2,1,0:T(2,128)S(1)} async-done(((f32[32,2,128]{2,1,0:T(2,128)}), f32[32,2,128]{2,1,0:T(2,128)S(1)}, u32[]{:S(2)}, u32[]{:S(2)}) %all-to-all-start) | async-done | bytes 32800 | tf_op jit(solution)/shard_map/all_to_all | solution.py:1767
  347.7 4.0 %apply.1 = (f32[4,96,192]{2,1,0:T(8,128)}, f32[2,24,768]{2,1,0:T(8,128)}, f32[2,176,192]{2,1,0:T(8,128)}, f32[96,768]{1,0:T(8,128)}, f32[96,768]{1,0:T(8,128)}, ...) custom-call(f32[32,2,128]{2,1,0:T(2,128)} %copy-done.68, ...), custom_call_target="tpu_custom_call" | custom-call | bytes 6549824 | tf_op jit(solution)/shard_map/apply/pallas_call | solution.py:960
  (292 shorter events, 61.6 us)
Async XLA Ops:
  2.4 21.1 %collective-permute-start = (bf16[160,768]{1,0:T(8,128)(2,1)S(1)}, bf16[160,768]{1,0:T(8,128)(2,1)S(1)}, u32[]{:S(2)}, u32[]{:S(2)}) collective-permute-start(bf16[160,768]{1,0:T(8,128)(2,1)S(1)} %constant_dynamic-update-slice_fusion), channel_id=1, source_target_pairs={{0,8},{1,9},{2,10},{3,11},{4,12},{5,13},{6,14},{7,15},{8,16},{9,17... | collective-permute-start | bytes 737288 | tf_op jit(solution)/shard_map/ppermute | solution.py:1023
  5.7 18.6 %collective-permute-start.1 = (bf16[160,768]{1,0:T(8,128)(2,1)S(1)}, bf16[160,768]{1,0:T(8,128)(2,1)S(1)}, u32[]{:S(2)}, u32[]{:S(2)}) collective-permute-start(bf16[160,768]{1,0:T(8,128)(2,1)S(1)} %constant_dynamic-update-slice_fusion), channel_id=1, source_target_pairs={{0,16},{1,17},{2,18},{3,19},{4,20},{5,21},{6,22},{7,23},{8,24},{9,... | collective-permute-start | bytes 737288 | tf_op jit(solution)/shard_map/ppermute | solution.py:1023
  8.3 16.1 %collective-permute-start.2 = (bf16[160,768]{1,0:T(8,128)(2,1)S(1)}, bf16[160,768]{1,0:T(8,128)(2,1)S(1)}, u32[]{:S(2)}, u32[]{:S(2)}) collective-permute-start(bf16[160,768]{1,0:T(8,128)(2,1)S(1)} %constant_dynamic-update-slice_fusion), channel_id=1, source_target_pairs={{0,24},{1,25},{2,26},{3,27},{4,28},{5,29},{6,30},{7,31},{8,0},{9,1... | collective-permute-start | bytes 737288 | tf_op jit(solution)/shard_map/ppermute | solution.py:1023
  24.6 18.6 %collective-permute-start.3 = (bf16[4,80,768]{2,1,0:T(8,128)(2,1)S(1)}, bf16[4,80,768]{2,1,0:T(8,128)(2,1)S(1)}, u32[]{:S(2)}, u32[]{:S(2)}) collective-permute-start(bf16[4,80,768]{2,1,0:T(8,128)(2,1)S(1)} %get-tuple-element.325), channel_id=1, source_target_pairs={{0,2},{1,3},{2,0},{3,1},{4,6},{5,7},{6,4},{7,5},{8,10},{9,11},{10,... | collective-permute-start | bytes 1474568 | tf_op jit(solution)/shard_map/ppermute | solution.py:1010
  26.2 17.1 %collective-permute-start.4 = (bf16[4,80,768]{2,1,0:T(8,128)(2,1)S(1)}, bf16[4,80,768]{2,1,0:T(8,128)(2,1)S(1)}, u32[]{:S(2)}, u32[]{:S(2)}) collective-permute-start(bf16[4,80,768]{2,1,0:T(8,128)(2,1)S(1)} %get-tuple-element.324), channel_id=1, source_target_pairs={{0,4},{1,5},{2,6},{3,7},{4,0},{5,1},{6,2},{7,3},{8,12},{9,13},{10,... | collective-permute-start | bytes 1474568 | tf_op jit(solution)/shard_map/ppermute | solution.py:1010
  27.7 11.3 %collective-permute-start.5 = (bf16[176,384]{1,0:T(8,128)(2,1)S(1)}, bf16[176,384]{1,0:T(8,128)(2,1)S(1)}, u32[]{:S(2)}, u32[]{:S(2)}) collective-permute-start(bf16[176,384]{1,0:T(8,128)(2,1)S(1)} %pad_maximum_fusion.18), channel_id=1, source_target_pairs={{0,8},{1,9},{2,10},{3,11},{4,12},{5,13},{6,14},{7,15},{8,16},{9,17... | collective-permute-start | bytes 405512 | tf_op jit(solution)/shard_map/ppermute | solution.py:1023
  33.4 9.7 %collective-permute-start.6 = (bf16[176,384]{1,0:T(8,128)(2,1)S(1)}, bf16[176,384]{1,0:T(8,128)(2,1)S(1)}, u32[]{:S(2)}, u32[]{:S(2)}) collective-permute-start(bf16[176,384]{1,0:T(8,128)(2,1)S(1)} %pad_maximum_fusion.18), channel_id=1, source_target_pairs={{0,16},{1,17},{2,18},{3,19},{4,20},{5,21},{6,22},{7,23},{8,24},{9,... | collective-permute-start | bytes 405512 | tf_op jit(solution)/shard_map/ppermute | solution.py:1023
  35.0 8.1 %collective-permute-start.7 = (bf16[176,384]{1,0:T(8,128)(2,1)S(1)}, bf16[176,384]{1,0:T(8,128)(2,1)S(1)}, u32[]{:S(2)}, u32[]{:S(2)}) collective-permute-start(bf16[176,384]{1,0:T(8,128)(2,1)S(1)} %pad_maximum_fusion.18), channel_id=1, source_target_pairs={{0,24},{1,25},{2,26},{3,27},{4,28},{5,29},{6,30},{7,31},{8,0},{9,1... | collective-permute-start | bytes 405512 | tf_op jit(solution)/shard_map/ppermute | solution.py:1023
  43.4 32.0 %collective-permute-start.9 = (bf16[2,4,80,768]{3,2,1,0:T(8,128)(2,1)S(1)}, bf16[2,4,80,768]{3,2,1,0:T(8,128)(2,1)S(1)}, u32[]{:S(2)}, u32[]{:S(2)}) collective-permute-start(bf16[2,4,80,768]{3,2,1,0:T(8,128)(2,1)S(1)} %get-tuple-element.321), channel_id=1, source_target_pairs={{0,2},{1,3},{2,0},{3,1},{4,6},{5,7},{6,4},{7,5},{8,10},{9,11},{10,... | collective-permute-start | bytes 2949128 | tf_op jit(solution)/shard_map/ppermute | solution.py:1010
  44.1 31.3 %collective-permute-start.8 = (bf16[2,4,80,768]{3,2,1,0:T(8,128)(2,1)S(1)}, bf16[2,4,80,768]{3,2,1,0:T(8,128)(2,1)S(1)}, u32[]{:S(2)}, u32[]{:S(2)}) collective-permute-start(bf16[2,4,80,768]{3,2,1,0:T(8,128)(2,1)S(1)} %get-tuple-element.319), channel_id=1, source_target_pairs={{0,4},{1,5},{2,6},{3,7},{4,0},{5,1},{6,2},{7,3},{8,12},{9,13},{10,... | collective-permute-start | bytes 2949128 | tf_op jit(solution)/shard_map/ppermute | solution.py:1010
  44.7 12.6 %collective-permute-start.12 = (bf16[192,768]{1,0:T(8,128)(2,1)S(1)}, bf16[192,768]{1,0:T(8,128)(2,1)S(1)}, u32[]{:S(2)}, u32[]{:S(2)}) collective-permute-start(bf16[192,768]{1,0:T(8,128)(2,1)S(1)} %pad_maximum_fusion.11), channel_id=1, source_target_pairs={{0,8},{1,9},{2,10},{3,11},{4,12},{5,13},{6,14},{7,15},{8,16},{9,17... | collective-permute-start | bytes 884744 | tf_op jit(solution)/shard_map/ppermute | solution.py:1023
  48.1 19.5 %collective-permute-start.13 = (bf16[192,768]{1,0:T(8,128)(2,1)S(1)}, bf16[192,768]{1,0:T(8,128)(2,1)S(1)}, u32[]{:S(2)}, u32[]{:S(2)}) collective-permute-start(bf16[192,768]{1,0:T(8,128)(2,1)S(1)} %pad_maximum_fusion.11), channel_id=1, source_target_pairs={{0,16},{1,17},{2,18},{3,19},{4,20},{5,21},{6,22},{7,23},{8,24},{9,... | collective-permute-start | bytes 884744 | tf_op jit(solution)/shard_map/ppermute | solution.py:1023
  49.8 19.2 %collective-permute-start.14 = (bf16[192,768]{1,0:T(8,128)(2,1)S(1)}, bf16[192,768]{1,0:T(8,128)(2,1)S(1)}, u32[]{:S(2)}, u32[]{:S(2)}) collective-permute-start(bf16[192,768]{1,0:T(8,128)(2,1)S(1)} %pad_maximum_fusion.11), channel_id=1, source_target_pairs={{0,24},{1,25},{2,26},{3,27},{4,28},{5,29},{6,30},{7,31},{8,0},{9,1... | collective-permute-start | bytes 884744 | tf_op jit(solution)/shard_map/ppermute | solution.py:1023
  57.3 18.0 %collective-permute-start.10 = (bf16[4,96,384]{2,1,0:T(8,128)(2,1)S(1)}, bf16[4,96,384]{2,1,0:T(8,128)(2,1)S(1)}, u32[]{:S(2)}, u32[]{:S(2)}) collective-permute-start(bf16[4,96,384]{2,1,0:T(8,128)(2,1)S(1)} %get-tuple-element.331), channel_id=1, source_target_pairs={{0,2},{1,3},{2,0},{3,1},{4,6},{5,7},{6,4},{7,5},{8,10},{9,11},{10,... | collective-permute-start | bytes 884744 | tf_op jit(solution)/shard_map/ppermute | solution.py:1010
  67.6 7.8 %collective-permute-start.11 = (bf16[4,80,384]{2,1,0:T(8,128)(2,1)S(1)}, bf16[4,80,384]{2,1,0:T(8,128)(2,1)S(1)}, u32[]{:S(2)}, u32[]{:S(2)}) collective-permute-start(bf16[4,80,384]{2,1,0:T(8,128)(2,1)S(1)} %get-tuple-element.329), channel_id=1, source_target_pairs={{0,4},{1,5},{2,6},{3,7},{4,0},{5,1},{6,2},{7,3},{8,12},{9,13},{10,... | collective-permute-start | bytes 737288 | tf_op jit(solution)/shard_map/ppermute | solution.py:1010
  80.3 28.7 %collective-permute-start.16 = (bf16[2,4,96,384]{3,2,1,0:T(8,128)(2,1)S(1)}, bf16[2,4,96,384]{3,2,1,0:T(8,128)(2,1)S(1)}, u32[]{:S(2)}, u32[]{:S(2)}) collective-permute-start(bf16[2,4,96,384]{3,2,1,0:T(8,128)(2,1)S(1)} %get-tuple-element.327), channel_id=1, source_target_pairs={{0,4},{1,5},{2,6},{3,7},{4,0},{5,1},{6,2},{7,3},{8,12},{9,13},{10,... | collective-permute-start | bytes 1769480 | tf_op jit(solution)/shard_map/ppermute | solution.py:1010
  83.0 25.9 %collective-permute-start.18 = (bf16[4,96,768]{2,1,0:T(8,128)(2,1)S(1)}, bf16[4,96,768]{2,1,0:T(8,128)(2,1)}, u32[]{:S(2)}, u32[]{:S(2)}) collective-permute-start(bf16[4,96,768]{2,1,0:T(8,128)(2,1)S(1)} %get-tuple-element.317), channel_id=1, source_target_pairs={{0,2},{1,3},{2,0},{3,1},{4,6},{5,7},{6,4},{7,5},{8,10},{9,11},{10,... | collective-permute-start | bytes 1769480 | tf_op jit(solution)/shard_map/ppermute | solution.py:1010
  84.5 24.5 %collective-permute-start.19 = (bf16[4,96,768]{2,1,0:T(8,128)(2,1)S(1)}, bf16[4,96,768]{2,1,0:T(8,128)(2,1)S(1)}, u32[]{:S(2)}, u32[]{:S(2)}) collective-permute-start(bf16[4,96,768]{2,1,0:T(8,128)(2,1)S(1)} %get-tuple-element.316), channel_id=1, source_target_pairs={{0,4},{1,5},{2,6},{3,7},{4,0},{5,1},{6,2},{7,3},{8,12},{9,13},{10,... | collective-permute-start | bytes 1769480 | tf_op jit(solution)/shard_map/ppermute | solution.py:1010
  85.1 23.8 %collective-permute-start.17 = (bf16[2,4,80,384]{3,2,1,0:T(8,128)(2,1)S(1)}, bf16[2,4,80,384]{3,2,1,0:T(8,128)(2,1)S(1)}, u32[]{:S(2)}, u32[]{:S(2)}) collective-permute-start(bf16[2,4,80,384]{3,2,1,0:T(8,128)(2,1)S(1)} %get-tuple-element.333), channel_id=1, source_target_pairs={{0,2},{1,3},{2,0},{3,1},{4,6},{5,7},{6,4},{7,5},{8,10},{9,11},{10,... | collective-permute-start | bytes 1474568 | tf_op jit(solution)/shard_map/ppermute | solution.py:1010
  111.7 28.4 %collective-permute-start.22 = (bf16[2,4,96,768]{3,2,1,0:T(8,128)(2,1)S(1)}, bf16[2,4,96,768]{3,2,1,0:T(8,128)(2,1)S(1)}, u32[]{:S(2)}, u32[]{:S(2)}) collective-permute-start(bf16[2,4,96,768]{3,2,1,0:T(8,128)(2,1)S(1)} %pad_maximum_fusion.4.down_first), channel_id=1, source_target_pairs={{0,2},{1,3},{2,0},{3,1},{4,6},{5,7},{6,4},{7,5},{8,10},{9,11},{10,... | collective-permute-start | bytes 3538952 | tf_op jit(solution)/shard_map/ppermute | solution.py:1010
  113.2 26.9 %collective-permute-start.24 = (bf16[2,4,96,768]{3,2,1,0:T(8,128)(2,1)S(1)}, bf16[2,4,96,768]{3,2,1,0:T(8,128)(2,1)S(1)}, u32[]{:S(2)}, u32[]{:S(2)}) collective-permute-start(bf16[2,4,96,768]{3,2,1,0:T(8,128)(2,1)S(1)} %pad_maximum_fusion.4.down_first), channel_id=1, source_target_pairs={{0,1},{1,0},{2,3},{3,2},{4,5},{5,4},{6,7},{7,6},{8,9},{9,8},{10,11... | collective-permute-start | bytes 3538952 | tf_op jit(solution)/shard_map/ppermute | solution.py:1010
  114.6 28.3 %collective-permute-start.21 = (bf16[2,4,96,768]{3,2,1,0:T(8,128)(2,1)S(1)}, bf16[2,4,96,768]{3,2,1,0:T(8,128)(2,1)S(1)}, u32[]{:S(2)}, u32[]{:S(2)}) collective-permute-start(bf16[2,4,96,768]{3,2,1,0:T(8,128)(2,1)S(1)} %pad_maximum_fusion.3.up_first), channel_id=1, source_target_pairs={{0,4},{1,5},{2,6},{3,7},{4,0},{5,1},{6,2},{7,3},{8,12},{9,13},{10,... | collective-permute-start | bytes 3538952 | tf_op jit(solution)/shard_map/ppermute | solution.py:1010
  115.9 27.0 %collective-permute-start.23 = (bf16[2,4,96,768]{3,2,1,0:T(8,128)(2,1)S(1)}, bf16[2,4,96,768]{3,2,1,0:T(8,128)(2,1)S(1)}, u32[]{:S(2)}, u32[]{:S(2)}) collective-permute-start(bf16[2,4,96,768]{3,2,1,0:T(8,128)(2,1)S(1)} %pad_maximum_fusion.3.up_first), channel_id=1, source_target_pairs={{0,1},{1,0},{2,3},{3,2},{4,5},{5,4},{6,7},{7,6},{8,9},{9,8},{10,11... | collective-permute-start | bytes 3538952 | tf_op jit(solution)/shard_map/ppermute | solution.py:1010
  166.9 22.1 %collective-permute-start.27 = (bf16[512,4608]{1,0:T(8,128)(2,1)}, bf16[512,4608]{1,0:T(8,128)(2,1)}, u32[]{:S(2)}, u32[]{:S(2)}) collective-permute-start(bf16[512,4608]{1,0:T(8,128)(2,1)} %get-tuple-element.182.rows), channel_id=1, source_target_pairs={{0,1},{1,0},{2,3},{3,2},{4,5},{5,4},{6,7},{7,6},{8,9},{9,8},{10,11... | collective-permute-start | bytes 14155784 | tf_op jit(solution)/shard_map/ppermute | solution.py:1010
  189.0 10.8 %collective-permute-start.28 = (bf16[2992,768]{1,0:T(8,128)(2,1)}, bf16[2992,768]{1,0:T(8,128)(2,1)S(1)}, u32[]{:S(2)}, u32[]{:S(2)}) collective-permute-start(bf16[2992,768]{1,0:T(8,128)(2,1)} %get-tuple-element.183), channel_id=1, source_target_pairs={{0,1},{1,0},{2,3},{3,2},{4,5},{5,4},{6,7},{7,6},{8,9},{9,8},{10,11... | collective-permute-start | bytes 13787144 | tf_op jit(solution)/shard_map/ppermute | solution.py:1010
  199.8 28.1 %collective-permute-start.29 = (bf16[2,4,96,768]{3,2,1,0:T(8,128)(2,1)S(1)}, bf16[2,4,96,768]{3,2,1,0:T(8,128)(2,1)S(1)}, u32[]{:S(2)}, u32[]{:S(2)}) collective-permute-start(bf16[2,4,96,768]{3,2,1,0:T(8,128)(2,1)S(1)} %get-tuple-element.195), channel_id=1, source_target_pairs={{0,4},{1,5},{2,6},{3,7},{4,0},{5,1},{6,2},{7,3},{8,12},{9,13},{10,... | collective-permute-start | bytes 3538952 | tf_op jit(solution)/shard_map/ppermute | solution.py:1010
  201.1 27.7 %collective-permute-start.30 = (bf16[2,4,96,768]{3,2,1,0:T(8,128)(2,1)S(1)}, bf16[2,4,96,768]{3,2,1,0:T(8,128)(2,1)S(1)}, u32[]{:S(2)}, u32[]{:S(2)}) collective-permute-start(bf16[2,4,96,768]{3,2,1,0:T(8,128)(2,1)S(1)} %get-tuple-element.196), channel_id=1, source_target_pairs={{0,2},{1,3},{2,0},{3,1},{4,6},{5,7},{6,4},{7,5},{8,10},{9,11},{10,... | collective-permute-start | bytes 3538952 | tf_op jit(solution)/shard_map/ppermute | solution.py:1010
  228.8 33.2 %collective-permute-start.32 = (bf16[2,4,72,768]{3,2,1,0:T(8,128)(2,1)S(1)}, bf16[2,4,72,768]{3,2,1,0:T(8,128)(2,1)S(1)}, u32[]{:S(2)}, u32[]{:S(2)}) collective-permute-start(bf16[2,4,72,768]{3,2,1,0:T(8,128)(2,1)S(1)} %get-tuple-element.208), channel_id=1, source_target_pairs={{0,2},{1,3},{2,0},{3,1},{4,6},{5,7},{6,4},{7,5},{8,10},{9,11},{10,... | collective-permute-start | bytes 2654216 | tf_op jit(solution)/shard_map/ppermute | solution.py:1010
  229.8 21.0 %collective-permute-start.34 = (bf16[4,96,768]{2,1,0:T(8,128)(2,1)S(1)}, bf16[4,96,768]{2,1,0:T(8,128)(2,1)S(1)}, u32[]{:S(2)}, u32[]{:S(2)}) collective-permute-start(bf16[4,96,768]{2,1,0:T(8,128)(2,1)S(1)} %fusion.1), channel_id=1, source_target_pairs={{0,4},{1,5},{2,6},{3,7},{4,0},{5,1},{6,2},{7,3},{8,12},{9,13},{10,... | collective-permute-start | bytes 1769480 | tf_op jit(solution)/shard_map/ppermute | solution.py:1010
  230.7 31.3 %collective-permute-start.31 = (bf16[2,4,64,768]{3,2,1,0:T(8,128)(2,1)S(1)}, bf16[2,4,64,768]{3,2,1,0:T(8,128)(2,1)S(1)}, u32[]{:S(2)}, u32[]{:S(2)}) collective-permute-start(bf16[2,4,64,768]{3,2,1,0:T(8,128)(2,1)S(1)} %get-tuple-element.207), channel_id=1, source_target_pairs={{0,4},{1,5},{2,6},{3,7},{4,0},{5,1},{6,2},{7,3},{8,12},{9,13},{10,... | collective-permute-start | bytes 2359304 | tf_op jit(solution)/shard_map/ppermute | solution.py:1010
  232.1 29.9 %collective-permute-start.33 = (bf16[4,96,768]{2,1,0:T(8,128)(2,1)S(1)}, bf16[4,96,768]{2,1,0:T(8,128)(2,1)S(1)}, u32[]{:S(2)}, u32[]{:S(2)}) collective-permute-start(bf16[4,96,768]{2,1,0:T(8,128)(2,1)S(1)} %fusion), channel_id=1, source_target_pairs={{0,2},{1,3},{2,0},{3,1},{4,6},{5,7},{6,4},{7,5},{8,10},{9,11},{10,... | collective-permute-start | bytes 1769480 | tf_op jit(solution)/shard_map/ppermute | solution.py:1010
  262.0 7.5 %collective-permute-start.35 = (bf16[528,3072]{1,0:T(8,128)(2,1)S(1)}, bf16[528,3072]{1,0:T(8,128)(2,1)S(1)}, u32[]{:S(2)}, u32[]{:S(2)}) collective-permute-start(bf16[528,3072]{1,0:T(8,128)(2,1)S(1)} %get-tuple-element.214.send), channel_id=1, source_target_pairs={{0,1},{1,0},{2,3},{3,2},{4,5},{5,4},{6,7},{7,6},{8,9},{9,8},{10,11... | collective-permute-start | bytes 9732104 | tf_op jit(solution)/shard_map/ppermute | solution.py:1010
  262.4 18.4 %collective-permute-start.41 = (bf16[4,72,768]{2,1,0:T(8,128)(2,1)S(1)}, bf16[4,72,768]{2,1,0:T(8,128)(2,1)S(1)}, u32[]{:S(2)}, u32[]{:S(2)}) collective-permute-start(bf16[4,72,768]{2,1,0:T(8,128)(2,1)S(1)} %fusion.4), channel_id=1, source_target_pairs={{0,4},{1,5},{2,6},{3,7},{4,0},{5,1},{6,2},{7,3},{8,12},{9,13},{10,... | collective-permute-start | bytes 1327112 | tf_op jit(solution)/shard_map/ppermute | solution.py:1010
  264.0 15.2 %collective-permute-start.36 = (bf16[192,768]{1,0:T(8,128)(2,1)S(1)}, bf16[192,768]{1,0:T(8,128)(2,1)S(1)}, u32[]{:S(2)}, u32[]{:S(2)}) collective-permute-start(bf16[192,768]{1,0:T(8,128)(2,1)S(1)} %pad_maximum_fusion.12), channel_id=1, source_target_pairs={{0,8},{1,9},{2,10},{3,11},{4,12},{5,13},{6,14},{7,15},{8,16},{9,17... | collective-permute-start | bytes 884744 | tf_op jit(solution)/shard_map/ppermute | solution.py:1023
  268.7 12.2 %collective-permute-start.40 = (bf16[4,64,768]{2,1,0:T(8,128)(2,1)S(1)}, bf16[4,64,768]{2,1,0:T(8,128)(2,1)S(1)}, u32[]{:S(2)}, u32[]{:S(2)}) collective-permute-start(bf16[4,64,768]{2,1,0:T(8,128)(2,1)S(1)} %fusion.7), channel_id=1, source_target_pairs={{0,2},{1,3},{2,0},{3,1},{4,6},{5,7},{6,4},{7,5},{8,10},{9,11},{10,... | collective-permute-start | bytes 1179656 | tf_op jit(solution)/shard_map/ppermute | solution.py:1010
  279.2 10.7 %collective-permute-start.39 = (bf16[192,768]{1,0:T(8,128)(2,1)S(1)}, bf16[192,768]{1,0:T(8,128)(2,1)S(1)}, u32[]{:S(2)}, u32[]{:S(2)}) collective-permute-start(bf16[192,768]{1,0:T(8,128)(2,1)S(1)} %fusion.2), channel_id=1, source_target_pairs={{0,8},{1,9},{2,10},{3,11},{4,12},{5,13},{6,14},{7,15},{8,16},{9,17... | collective-permute-start | bytes 884744 | tf_op jit(solution)/shard_map/ppermute | solution.py:1023
  279.2 25.0 %collective-permute-start.38 = (bf16[2,4,56,768]{3,2,1,0:T(8,128)(2,1)S(1)}, bf16[2,4,56,768]{3,2,1,0:T(8,128)(2,1)S(1)}, u32[]{:S(2)}, u32[]{:S(2)}) collective-permute-start(bf16[2,4,56,768]{3,2,1,0:T(8,128)(2,1)S(1)} %get-tuple-element.221), channel_id=1, source_target_pairs={{0,2},{1,3},{2,0},{3,1},{4,6},{5,7},{6,4},{7,5},{8,10},{9,11},{10,... | collective-permute-start | bytes 2064392 | tf_op jit(solution)/shard_map/ppermute | solution.py:1010
  280.1 24.2 %collective-permute-start.37 = (bf16[2,4,48,768]{3,2,1,0:T(8,128)(2,1)S(1)}, bf16[2,4,48,768]{3,2,1,0:T(8,128)(2,1)S(1)}, u32[]{:S(2)}, u32[]{:S(2)}) collective-permute-start(bf16[2,4,48,768]{3,2,1,0:T(8,128)(2,1)S(1)} %get-tuple-element.220), channel_id=1, source_target_pairs={{0,4},{1,5},{2,6},{3,7},{4,0},{5,1},{6,2},{7,3},{8,12},{9,13},{10,... | collective-permute-start | bytes 1769480 | tf_op jit(solution)/shard_map/ppermute | solution.py:1010
  289.9 14.3 %collective-permute-start.43 = (bf16[192,768]{1,0:T(8,128)(2,1)S(1)}, bf16[192,768]{1,0:T(8,128)(2,1)S(1)}, u32[]{:S(2)}, u32[]{:S(2)}) collective-permute-start(bf16[192,768]{1,0:T(8,128)(2,1)S(1)} %fusion.3), channel_id=1, source_target_pairs={{0,8},{1,9},{2,10},{3,11},{4,12},{5,13},{6,14},{7,15},{8,16},{9,17... | collective-permute-start | bytes 884744 | tf_op jit(solution)/shard_map/ppermute | solution.py:1023
  290.4 13.9 %collective-permute-start.42 = (bf16[136,768]{1,0:T(8,128)(2,1)S(1)}, bf16[136,768]{1,0:T(8,128)(2,1)S(1)}, u32[]{:S(2)}, u32[]{:S(2)}) collective-permute-start(bf16[136,768]{1,0:T(8,128)(2,1)S(1)} %pad_maximum_fusion.13), channel_id=1, source_target_pairs={{0,8},{1,9},{2,10},{3,11},{4,12},{5,13},{6,14},{7,15},{8,16},{9,17... | collective-permute-start | bytes 626696 | tf_op jit(solution)/shard_map/ppermute | solution.py:1023
  304.4 10.5 %collective-permute-start.46 = (bf16[4,56,768]{2,1,0:T(8,128)(2,1)S(1)}, bf16[4,56,768]{2,1,0:T(8,128)(2,1)S(1)}, u32[]{:S(2)}, u32[]{:S(2)}) collective-permute-start(bf16[4,56,768]{2,1,0:T(8,128)(2,1)S(1)} %fusion.8), channel_id=1, source_target_pairs={{0,4},{1,5},{2,6},{3,7},{4,0},{5,1},{6,2},{7,3},{8,12},{9,13},{10,... | collective-permute-start | bytes 1032200 | tf_op jit(solution)/shard_map/ppermute | solution.py:1010
  304.8 10.0 %collective-permute-start.45 = (bf16[4,48,768]{2,1,0:T(8,128)(2,1)S(1)}, bf16[4,48,768]{2,1,0:T(8,128)(2,1)S(1)}, u32[]{:S(2)}, u32[]{:S(2)}) collective-permute-start(bf16[4,48,768]{2,1,0:T(8,128)(2,1)S(1)} %fusion.11), channel_id=1, source_target_pairs={{0,2},{1,3},{2,0},{3,1},{4,6},{5,7},{6,4},{7,5},{8,10},{9,11},{10,... | collective-permute-start | bytes 884744 | tf_op jit(solution)/shard_map/ppermute | solution.py:1010
  305.7 9.1 %collective-permute-start.44 = (bf16[136,768]{1,0:T(8,128)(2,1)S(1)}, bf16[136,768]{1,0:T(8,128)(2,1)S(1)}, u32[]{:S(2)}, u32[]{:S(2)}) collective-permute-start(bf16[136,768]{1,0:T(8,128)(2,1)S(1)} %fusion.6), channel_id=1, source_target_pairs={{0,8},{1,9},{2,10},{3,11},{4,12},{5,13},{6,14},{7,15},{8,16},{9,17... | collective-permute-start | bytes 626696 | tf_op jit(solution)/shard_map/ppermute | solution.py:1023
  315.1 8.6 %collective-permute-start.48 = (bf16[104,768]{1,0:T(8,128)(2,1)S(1)}, bf16[104,768]{1,0:T(8,128)(2,1)S(1)}, u32[]{:S(2)}, u32[]{:S(2)}) collective-permute-start(bf16[104,768]{1,0:T(8,128)(2,1)S(1)} %pad_maximum_fusion.14), channel_id=1, source_target_pairs={{0,24},{1,25},{2,26},{3,27},{4,28},{5,29},{6,30},{7,31},{8,0},{9,1... | collective-permute-start | bytes 479240 | tf_op jit(solution)/shard_map/ppermute | solution.py:1023
  315.2 16.3 %collective-permute-start.49 = (bf16[104,768]{1,0:T(8,128)(2,1)S(1)}, bf16[104,768]{1,0:T(8,128)(2,1)S(1)}, u32[]{:S(2)}, u32[]{:S(2)}) collective-permute-start(bf16[104,768]{1,0:T(8,128)(2,1)S(1)} %pad_maximum_fusion.15), channel_id=1, source_target_pairs={{0,16},{1,17},{2,18},{3,19},{4,20},{5,21},{6,22},{7,23},{8,24},{9,... | collective-permute-start | bytes 479240 | tf_op jit(solution)/shard_map/ppermute | solution.py:1023
  315.3 16.2 %collective-permute-start.50 = (bf16[104,768]{1,0:T(8,128)(2,1)S(1)}, bf16[104,768]{1,0:T(8,128)(2,1)S(1)}, u32[]{:S(2)}, u32[]{:S(2)}) collective-permute-start(bf16[104,768]{1,0:T(8,128)(2,1)S(1)} %pad_maximum_fusion.16), channel_id=1, source_target_pairs={{0,8},{1,9},{2,10},{3,11},{4,12},{5,13},{6,14},{7,15},{8,16},{9,17... | collective-permute-start | bytes 479240 | tf_op jit(solution)/shard_map/ppermute | solution.py:1023
  317.4 14.3 %collective-permute-start.47 = (bf16[136,768]{1,0:T(8,128)(2,1)S(1)}, bf16[136,768]{1,0:T(8,128)(2,1)S(1)}, u32[]{:S(2)}, u32[]{:S(2)}) collective-permute-start(bf16[136,768]{1,0:T(8,128)(2,1)S(1)} %fusion.5), channel_id=1, source_target_pairs={{0,8},{1,9},{2,10},{3,11},{4,12},{5,13},{6,14},{7,15},{8,16},{9,17... | collective-permute-start | bytes 626696 | tf_op jit(solution)/shard_map/ppermute | solution.py:1023
  337.3 9.8 %all-to-all-start = ((f32[32,2,128]{2,1,0:T(2,128)}), f32[32,2,128]{2,1,0:T(2,128)S(1)}, u32[]{:S(2)}, u32[]{:S(2)}) async-start(f32[32,2,128]{2,1,0:T(2,128)} %broadcast_in_dim.18), calls=%async_computation | async-start | bytes 65536 | tf_op jit(solution)/shard_map/all_to_all | solution.py:1767
  (80 other events, 505.8 us)
where the time goes:
time: 358 us; the launch traced here: 353 us
  Pallas kernels  126 us (35%)
  waiting for transfers between devices  109 us (30%)
  starting transfers between devices  59 us (16%)
  local copies, waits for them, and re-layouts  46.5 us (13%)
  other arithmetic  10.2 us (3%)
    ppermute x18, waiting for transfers between devices, hop_z(): lax.ppermute(values, AXES, [(i, (i + step) % self.count) for i in range(s...  68.9 us
    pallas_call x7, Pallas kernels, local_call(): pl.pallas_call(kernel, out_shape=tuple(out_shapes), in_specs=[SCALARS] *...  42.3 us
    ppermute x33, waiting for transfers between devices, hop(): lax.ppermute(values, AXES, [(i, i ^ flip) for i in range(self.count)])  34 us
    ppermute x18, starting transfers between devices, hop_z(): lax.ppermute(values, AXES, [(i, (i + step) % self.count) for i in range(s...  29.6 us
    ppermute x33, starting transfers between devices, hop(): lax.ppermute(values, AXES, [(i, i ^ flip) for i in range(self.count)])  26.8 us
    unnamed x159, local copies, waits for them, and re-layouts  26.2 us
    pallas_call x1, Pallas kernels, look(): pl.pallas_call(look_kernel, out_shape=(shape_of(rows, 2 * features), shap...  21.3 us
    pallas_call x1, Pallas kernels, feed(): pl.pallas_call(feed_kernel, out_shape=(shape_of(rows, features), shape_of...  19.2 us
  transfers between devices with their start and end apart: 52, of which 21 were waited for; matrix products, arithmetic and copies ran while one was open for 7% of the time, Pallas kernels for 28%

commit v1 on v0

--- a/solution.py
+++ b/solution.py
@@ -1502,7 +1502,6 @@
     feed_first = moves.fold_first(feed_grads)
     image_grads = image_grad(feats_place, feats, cross_keep, cross_other)
     one_query_grad, image_grads, feed_first = tie(one_query_grad, image_grads, feed_first)
-    feed_second = moves.fold_second(feed_grads, feed_first)
     image_first = moves.fold_first(image_grads)
     input_grad, self_keep, self_send, norm_total = self_backward(
         lengths,
@@ -1517,24 +1516,25 @@
         w_self_out,
         norm_grads,
     )
-    self_send, image_first, feed_second = tie(self_send, image_first, feed_second)
+    self_send, image_first, feed_first = tie(self_send, image_first, feed_first)
     self_other = moves.hop_core(self_send)
+    feed_second = moves.fold_second(feed_grads, feed_first)
+    self_other, feed_first, image_first = tie(self_other, feed_first, image_first)
+    image_second = moves.fold_second(image_grads, image_first)
+    self_grads = self_grad(place, self_keep, self_send, self_other, norm_total)
+    self_first = moves.fold_first(self_grads)
     feed_kept = moves.kept(feed_grads, feed_first, feed_second)
     feed_other = moves.ring_z(feed_kept, 1)
-    image_second = moves.fold_second(image_grads, image_first)
-    self_grads = self_grad(place, self_keep, self_send, self_other, norm_total)
-    self_grads, feed_other = tie(self_grads, feed_other)
-    self_first = moves.fold_first(self_grads)
+    image_second, feed_other = tie(image_second, feed_other)
+    image_kept = moves.kept(image_grads, image_first, image_second)
     feed_other = moves.ring_z(feed_kept, 2, feed_other)
-    feed_other, image_second = tie(feed_other, image_second)
-    image_kept = moves.kept(image_grads, image_first, image_second)
-    feed_other = moves.ring_z(feed_kept, 3, feed_other)
     image_other = moves.ring_z(image_kept, 1)
     self_first, image_other, feed_other = tie(self_first, image_other, feed_other)
     self_second = moves.fold_second(self_grads, self_first)
+    feed_other = moves.ring_z(feed_kept, 3, feed_other)
     image_other = moves.ring_z(image_kept, 2, image_other)
+    self_second, image_other, feed_other = tie(self_second, image_other, feed_other)
     feed_sum = moves.finish(feed_kept, [feed_other])
-    image_other, self_second = tie(image_other, self_second)
     image_other = moves.ring_z(image_kept, 3, image_other)
     self_kept = moves.kept(self_grads, self_first, self_second)
     self_others = moves.fold_z(self_kept)

time: 358 us -> 353 us (0.986)
  waiting for transfers between devices: 109 us -> 93.2 us
  starting transfers between devices: 59 us -> 68.7 us
    ppermute x18, waiting for transfers between devices: 68.9 us -> 44.7 us  [hop_z(): lax.ppermute(values, AXES, [(i, (i + step) % self.count) for i in range(s...]
    ppermute x33, waiting for transfers between devices: 34 us -> 41.9 us  [hop(): lax.ppermute(values, AXES, [(i, i ^ flip) for i in range(self.count)])]
    ppermute x18, starting transfers between devices: 29.6 us -> 37.1 us  [hop_z(): lax.ppermute(values, AXES, [(i, (i + step) % self.count) for i in range(s...]
  transfers between devices with their start and end apart: 52 -> 52, of which waited for: 21 -> 23; matrix products, arithmetic and copies ran while one was open for 7% -> 7% of each run, Pallas kernels for 28% -> 29%
where the time goes in v1:
time: 353 us; the launch traced here: 349 us
  Pallas kernels  126 us (36%)
  waiting for transfers between devices  93.2 us (26%)
  starting transfers between devices  68.7 us (19%)
  local copies, waits for them, and re-layouts  48.6 us (14%)
  other arithmetic  10.2 us (3%)
    ppermute x18, waiting for transfers between devices, hop_z(): lax.ppermute(values, AXES, [(i, (i + step) % self.count) for i in range(s...  44.7 us
    pallas_call x7, Pallas kernels, local_call(): pl.pallas_call(kernel, out_shape=tuple(out_shapes), in_specs=[SCALARS] *...  42.3 us
    ppermute x33, waiting for transfers between devices, hop(): lax.ppermute(values, AXES, [(i, i ^ flip) for i in range(self.count)])  41.9 us
    ppermute x18, starting transfers between devices, hop_z(): lax.ppermute(values, AXES, [(i, (i + step) % self.count) for i in range(s...  37.1 us
    ppermute x33, starting transfers between devices, hop(): lax.ppermute(values, AXES, [(i, i ^ flip) for i in range(self.count)])  29 us
    unnamed x159, local copies, waits for them, and re-layouts  28.3 us
    pallas_call x1, Pallas kernels, look(): pl.pallas_call(look_kernel, out_shape=(shape_of(rows, 2 * features), shap...  21.3 us
    pallas_call x1, Pallas kernels, image_grad(): pl.pallas_call(functools.partial(image_grad_kernel, items // 2 * QUERIES)...  19.2 us
  transfers between devices with their start and end apart: 52, of which 23 were waited for; matrix products, arithmetic and copies ran while one was open for 7% of the time, Pallas kernels for 29%

profile of v1, /device:TPU:0, one launch (start us, length us, event | category | flops | bytes accessed | tf_op | source)
XLA Modules:
  0.0 348.8 jit_solution(9177220530530696754)
XLA Ops:
  2.4 3.3 collective-permute-start
  5.7 2.6 collective-permute-start.1
  9.6 5.9 %constant_dynamic-slice_fusion.1 = bf16[16,257,1408]{2,0,1:T(8,128)(2,1)S(1)} fusion(bf16[32,257,1408]{2,0,1:T(8,128)(2,1)} %param.23, s32[]{:T(128)S(6)} %select_n.51), kind=kLoop, calls=%fused_computation.117 | loop fusion | bytes 23158788 | tf_op jit(solution)/shard_map/dynamic_slice | solution.py:1693
  15.5 7.8 %copy.50.feats = bf16[16,257,1408]{2,1,0:T(8,128)(2,1)} copy(bf16[16,257,1408]{2,0,1:T(8,128)(2,1)S(1)} %constant_dynamic-slice_fusion.1) | data formatting | bytes 23158784 | tf_op jit(solution)/shard_map/optimization_barrier | solution.py:1130
  27.7 5.7 %collective-permute-start.5 = (bf16[176,384]{1,0:T(8,128)(2,1)S(1)}, bf16[176,384]{1,0:T(8,128)(2,1)S(1)}, u32[]{:S(2)}, u32[]{:S(2)}) collective-permute-start(bf16[176,384]{1,0:T(8,128)(2,1)S(1)} %pad_maximum_fusion.18), channel_id=1, source_target_pairs={{0,8},{1,9},{2,10},{3,11},{4,12},{5,13},{6,14},{7,15},{8,16},{9,17... | collective-permute-start | bytes 405512 | tf_op jit(solution)/shard_map/ppermute | solution.py:1023
  33.4 1.6 collective-permute-start.6
  35.8 3.1 collective-permute-done.5
  38.9 4.2 %collective-permute-done.6 = bf16[176,384]{1,0:T(8,128)(2,1)S(1)} collective-permute-done((bf16[176,384]{1,0:T(8,128)(2,1)S(1)}, bf16[176,384]{1,0:T(8,128)(2,1)S(1)}, u32[]{:S(2)}, u32[]{:S(2)}) %collective-permute-start.6) | collective-permute-done | bytes 135200 | tf_op jit(solution)/shard_map/ppermute | solution.py:1023
  44.7 3.4 collective-permute-start.12
  48.1 1.7 collective-permute-start.13
  51.2 6.1 %collective-permute-done.12 = bf16[192,768]{1,0:T(8,128)(2,1)S(1)} collective-permute-done((bf16[192,768]{1,0:T(8,128)(2,1)S(1)}, bf16[192,768]{1,0:T(8,128)(2,1)S(1)}, u32[]{:S(2)}, u32[]{:S(2)}) %collective-permute-start.12) | collective-permute-done | bytes 294944 | tf_op jit(solution)/shard_map/ppermute | solution.py:1023
  58.8 8.7 %collective-permute-done.13 = bf16[192,768]{1,0:T(8,128)(2,1)S(1)} collective-permute-done((bf16[192,768]{1,0:T(8,128)(2,1)S(1)}, bf16[192,768]{1,0:T(8,128)(2,1)S(1)}, u32[]{:S(2)}, u32[]{:S(2)}) %collective-permute-start.13) | collective-permute-done | bytes 294944 | tf_op jit(solution)/shard_map/ppermute | solution.py:1023
  70.2 5.1 %collective-permute-done.11 = bf16[4,80,384]{2,1,0:T(8,128)(2,1)S(1)} collective-permute-done((bf16[4,80,384]{2,1,0:T(8,128)(2,1)S(1)}, bf16[4,80,384]{2,1,0:T(8,128)(2,1)S(1)}, u32[]{:S(2)}, u32[]{:S(2)}) %collective-permute-start.11) | collective-permute-done | bytes 245792 | tf_op jit(solution)/shard_map/ppermute | solution.py:1010
  76.9 2.2 copy.46
  80.3 1.6 collective-permute-start.16
  86.2 12.2 %self_forward.1 = (f32[512,768]{1,0:T(8,128)S(1)}, bf16[512,2304]{1,0:T(8,128)(2,1)S(1)}, bf16[512,768]{1,0:T(8,128)(2,1)S(1)}, bf16[768,2304]{1,0:T(8,128)(2,1)...) custom-call(s32[16]{0:T(128)S(1)} %pad_add_fusion.place, ...), custom_call_target="tpu_custom_call" | custom-call | flops 3019898880 | bytes 20471808 | tf_op jit(solution)/shard_map/self_forward/pallas_call | solution.py:960
  98.4 1.7 copy-done.47
  103.4 5.5 %collective-permute-done.17 = bf16[2,4,80,384]{3,2,1,0:T(8,128)(2,1)S(1)} collective-permute-done((bf16[2,4,80,384]{3,2,1,0:T(8,128)(2,1)S(1)}, bf16[2,4,80,384]{3,2,1,0:T(8,128)(2,1)S(1)}, u32[]{:S(2)}, u32[]{:S(2)}) %collective-permute-start.17) | collective-permute-done | bytes 491552 | tf_op jit(solution)/shard_map/ppermute | solution.py:1010
  116.0 21.3 %look.1 = (bf16[2176,1536]{1,0:T(8,128)(2,1)}, f32[256,768]{1,0:T(8,128)S(1)}, bf16[256,768]{1,0:T(8,128)(2,1)S(1)}, bf16[256,768]{1,0:T(8,128)(2,1)S(1)}) custom-call(s32[17]{0:T(128)S(1)} %pad_add_fusion.1.place, bf16[16,257,1408]{2,1,0:T(8,128)(2,1)} %copy.50.feats, bf16[16,176,384]{2,1,0:T(8,128)(2,1)S(1)} %bitcast.225, ...), custom_call_target="tpu_custom_call" | custom-call | flops 11765022720 | bytes 17137664 | tf_op jit(solution)/shard_map/look/pallas_call | solution.py:1170
  140.1 2.8 collective-permute-done.21.up_last
  143.5 3.1 collective-permute-done.25.up_last_other
  147.7 19.1 %feed.1 = (bf16[512,768]{1,0:T(8,128)(2,1)}, f32[512,768]{1,0:T(8,128)}, bf16[512,3072]{1,0:T(8,128)(2,1)}, bf16[512,4608]{1,0:T(8,128)(2,1)}, f32[8,768]{1,0:T(8,128)}) custom-call(s32[16]{0:T(128)} %copy-done.42, s32[8]{0:T(128)} %copy-done.44, f32[8,768]{1,0:T(8,128)} %copy-done.33, f32[512,768]{1,0:T(8,128)} %copy-done.4, f32[256,768]{1,0:T(8,128)} %copy-done.17, ...), custom_call_target="tpu_custom_call" | custom-call | flops 9663676416 | bytes 9437184 | tf_op jit(solution)/shard_map/feed/pallas_call | solution.py:1211
  171.1 15.6 %cross_backward.1 = (bf16[2992,768]{1,0:T(8,128)(2,1)S(1)}, bf16[2992,768]{1,0:T(8,128)(2,1)}, f32[256,768]{1,0:T(8,128)S(1)}, f32[8,768]{1,0:T(8,128)S(1)}) custom-call(f32[512,768]{1,0:T(8,128)S(1)} %copy-done.7, f32[512,768]{1,0:T(8,128)S(1)} %copy-done.6, f32[256,768]{1,0:T(8,128)S(1)} %copy-done.18, f32[8,768]{1,0:T(8,128)S(1)} %copy-done.34, ...), custom_call_target="tpu_custom_call" | custom-call | flops 3019898880 | bytes 27574272 | tf_op jit(solution)/shard_map/cross_backward/pallas_call | solution.py:1313
  186.7 2.1 copy-done.38
  189.2 1.9 copy-done.46
  191.1 8.5 %feed_grad.1 = (bf16[2,4,96,768]{3,2,1,0:T(8,128)(2,1)S(1)}, bf16[2,4,96,768]{3,2,1,0:T(8,128)(2,1)S(1)}, bf16[2,4,96,768]{3,2,1,0:T(8,128)(2,1)S(1)}, bf16[2,4,96,768]{3,2,1,0:T(8,128)(2,1)S(1)}) custom-call(s32[16]{0:T(128)S(1)} %copy-done.43, bf16[512,3072]{1,0:T(8,128)(2,1)S(1)} %copy-done.46, bf16[512,4608]{1,0:T(8,128)(2,1)S(1)} %copy-done.37, ...), custom_call_target="tpu_custom_call" | custom-call | flops 4831838208 | bytes 9437184 | tf_op jit(solution)/shard_map/feed_grad/pallas_call | solution.py:1261
  201.7 2.3 copy-done.39
  204.0 19.2 %image_grad.1 = (bf16[2,4,64,768]{3,2,1,0:T(8,128)(2,1)S(1)}, bf16[2,4,64,768]{3,2,1,0:T(8,128)(2,1)S(1)}, bf16[2,4,72,768]{3,2,1,0:T(8,128)(2,1)S(1)}, bf16[2,4,72,768]{3,2,1,0:T(8,128)(2,1)S(1)}) custom-call(s32[17]{0:T(128)S(1)} %pad_add_fusion.1.place, bf16[16,257,1408]{2,1,0:T(8,128)(2,1)} %copy.50.feats, bf16[2992,768]{1,0:T(8,128)(2,1)S(1)} %copy-done.39, ...), custom_call_target="tpu_custom_call" | custom-call | flops 9412018176 | bytes 18939904 | tf_op jit(solution)/shard_map/image_grad/pallas_call | solution.py:1346
  223.2 4.6 %collective-permute-done.29 = bf16[2,4,96,768]{3,2,1,0:T(8,128)(2,1)S(1)} collective-permute-done((bf16[2,4,96,768]{3,2,1,0:T(8,128)(2,1)S(1)}, bf16[2,4,96,768]{3,2,1,0:T(8,128)(2,1)S(1)}, u32[]{:S(2)}, u32[]{:S(2)}) %collective-permute-start.29) | collective-permute-done | bytes 1179680 | tf_op jit(solution)/shard_map/ppermute | solution.py:1010
  230.3 2.0 copy-done.48
  234.7 15.7 %self_backward.1 = (bf16[512,768]{1,0:T(8,128)(2,1)}, bf16[512,1536]{1,0:T(8,128)(2,1)S(1)}, bf16[528,3072]{1,0:T(8,128)(2,1)S(1)}, f32[8,768]{1,0:T(8,128)S(1)}) custom-call(s32[8]{0:T(128)S(1)} %copy-done.45, f32[256,768]{1,0:T(8,128)S(1)} %get-tuple-element.198.one_query_grad, f32[512,768]{1,0:T(8,128)S(1)} %copy-done.8, f32[512,768]{1,0:T(8,128)S(1)} %copy-done.6, ...), custom_call_target="tpu_custom_call" | custom-call | flops 4831838208 | bytes 18259968 | tf_op jit(solution)/shard_map/self_backward/pallas_call | solution.py:960
  253.6 2.6 collective-permute-done.33.other
  259.1 7.7 %collective-permute-done.34 = bf16[4,96,768]{2,1,0:T(8,128)(2,1)S(1)} collective-permute-done((bf16[4,96,768]{2,1,0:T(8,128)(2,1)S(1)}, bf16[4,96,768]{2,1,0:T(8,128)(2,1)S(1)}, u32[]{:S(2)}, u32[]{:S(2)}) %collective-permute-start.34) | collective-permute-done | bytes 589856 | tf_op jit(solution)/shard_map/ppermute | solution.py:1010
  267.0 1.6 collective-permute-done.35
  268.8 4.6 %collective-permute-start.40 = (bf16[192,768]{1,0:T(8,128)(2,1)S(1)}, bf16[192,768]{1,0:T(8,128)(2,1)S(1)}, u32[]{:S(2)}, u32[]{:S(2)}) collective-permute-start(bf16[192,768]{1,0:T(8,128)(2,1)S(1)} %pad_maximum_fusion.12), channel_id=1, source_target_pairs={{0,8},{1,9},{2,10},{3,11},{4,12},{5,13},{6,14},{7,15},{8,16},{9,17... | collective-permute-start | bytes 884744 | tf_op jit(solution)/shard_map/ppermute | solution.py:1023
  273.4 5.9 %self_grad.1 = (bf16[2,4,48,768]{3,2,1,0:T(8,128)(2,1)S(1)}, bf16[2,4,48,768]{3,2,1,0:T(8,128)(2,1)S(1)}, bf16[2,4,56,768]{3,2,1,0:T(8,128)(2,1)S(1)}, bf16[2,4,56,768]{3,2,1,0:T(8,128)(2,1)S(1)}) custom-call(s32[16]{0:T(128)S(1)} %copy-done.43, bf16[512,1536]{1,0:T(8,128)(2,1)S(1)} %get-tuple-element.219.keep, ...), custom_call_target="tpu_custom_call" | custom-call | flops 2415919104 | bytes 10641408 | tf_op jit(solution)/shard_map/self_grad/pallas_call | solution.py:960
  283.1 3.0 collective-permute-start.41
  286.0 7.2 %collective-permute-done.36 = bf16[2,4,48,768]{3,2,1,0:T(8,128)(2,1)S(1)} collective-permute-done((bf16[2,4,48,768]{3,2,1,0:T(8,128)(2,1)S(1)}, bf16[2,4,48,768]{3,2,1,0:T(8,128)(2,1)S(1)}, u32[]{:S(2)}, u32[]{:S(2)}) %collective-permute-start.36) | collective-permute-done | bytes 589856 | tf_op jit(solution)/shard_map/ppermute | solution.py:1010
  293.2 2.6 collective-permute-done.41
  298.2 3.2 collective-permute-start.45
  301.4 7.4 %collective-permute-done.45 = bf16[136,768]{1,0:T(8,128)(2,1)S(1)} collective-permute-done((bf16[136,768]{1,0:T(8,128)(2,1)S(1)}, bf16[136,768]{1,0:T(8,128)(2,1)S(1)}, u32[]{:S(2)}, u32[]{:S(2)}) %collective-permute-start.45) | collective-permute-done | bytes 208928 | tf_op jit(solution)/shard_map/ppermute | solution.py:1023
  309.2 3.9 %collective-permute-start.48 = (bf16[104,768]{1,0:T(8,128)(2,1)S(1)}, bf16[104,768]{1,0:T(8,128)(2,1)S(1)}, u32[]{:S(2)}, u32[]{:S(2)}) collective-permute-start(bf16[104,768]{1,0:T(8,128)(2,1)S(1)} %pad_maximum_fusion.14), channel_id=1, source_target_pairs={{0,24},{1,25},{2,26},{3,27},{4,28},{5,29},{6,30},{7,31},{8,0},{9,1... | collective-permute-start | bytes 479240 | tf_op jit(solution)/shard_map/ppermute | solution.py:1023
  313.9 1.7 feed_update.1
  315.6 2.2 collective-permute-done.48
  317.8 9.1 %collective-permute-done.49 = bf16[104,768]{1,0:T(8,128)(2,1)S(1)} collective-permute-done((bf16[104,768]{1,0:T(8,128)(2,1)S(1)}, bf16[104,768]{1,0:T(8,128)(2,1)S(1)}, u32[]{:S(2)}, u32[]{:S(2)}) %collective-permute-start.49) | collective-permute-done | bytes 159776 | tf_op jit(solution)/shard_map/ppermute | solution.py:1023
  332.7 2.6 all-to-all-start
  335.9 6.7 %all-to-all-done.squares = f32[32,2,128]{2,1,0:T(2,128)S(1)} async-done(((f32[32,2,128]{2,1,0:T(2,128)}), f32[32,2,128]{2,1,0:T(2,128)S(1)}, u32[]{:S(2)}, u32[]{:S(2)}) %all-to-all-start) | async-done | bytes 32800 | tf_op jit(solution)/shard_map/all_to_all | solution.py:1767
  343.1 4.0 %apply.1 = (f32[4,96,192]{2,1,0:T(8,128)}, f32[2,24,768]{2,1,0:T(8,128)}, f32[2,176,192]{2,1,0:T(8,128)}, f32[96,768]{1,0:T(8,128)}, f32[96,768]{1,0:T(8,128)}, ...) custom-call(f32[32,2,128]{2,1,0:T(2,128)} %copy-done.68, ...), custom_call_target="tpu_custom_call" | custom-call | bytes 6549824 | tf_op jit(solution)/shard_map/apply/pallas_call | solution.py:960
  (292 shorter events, 70.3 us)
Async XLA Ops:
  2.4 21.1 %collective-permute-start = (bf16[160,768]{1,0:T(8,128)(2,1)S(1)}, bf16[160,768]{1,0:T(8,128)(2,1)S(1)}, u32[]{:S(2)}, u32[]{:S(2)}) collective-permute-start(bf16[160,768]{1,0:T(8,128)(2,1)S(1)} %constant_dynamic-update-slice_fusion), channel_id=1, source_target_pairs={{0,8},{1,9},{2,10},{3,11},{4,12},{5,13},{6,14},{7,15},{8,16},{9,17... | collective-permute-start | bytes 737288 | tf_op jit(solution)/shard_map/ppermute | solution.py:1023
  5.7 18.6 %collective-permute-start.1 = (bf16[160,768]{1,0:T(8,128)(2,1)S(1)}, bf16[160,768]{1,0:T(8,128)(2,1)S(1)}, u32[]{:S(2)}, u32[]{:S(2)}) collective-permute-start(bf16[160,768]{1,0:T(8,128)(2,1)S(1)} %constant_dynamic-update-slice_fusion), channel_id=1, source_target_pairs={{0,16},{1,17},{2,18},{3,19},{4,20},{5,21},{6,22},{7,23},{8,24},{9,... | collective-permute-start | bytes 737288 | tf_op jit(solution)/shard_map/ppermute | solution.py:1023
  8.3 16.1 %collective-permute-start.2 = (bf16[160,768]{1,0:T(8,128)(2,1)S(1)}, bf16[160,768]{1,0:T(8,128)(2,1)S(1)}, u32[]{:S(2)}, u32[]{:S(2)}) collective-permute-start(bf16[160,768]{1,0:T(8,128)(2,1)S(1)} %constant_dynamic-update-slice_fusion), channel_id=1, source_target_pairs={{0,24},{1,25},{2,26},{3,27},{4,28},{5,29},{6,30},{7,31},{8,0},{9,1... | collective-permute-start | bytes 737288 | tf_op jit(solution)/shard_map/ppermute | solution.py:1023
  24.6 18.6 %collective-permute-start.3 = (bf16[4,80,768]{2,1,0:T(8,128)(2,1)S(1)}, bf16[4,80,768]{2,1,0:T(8,128)(2,1)S(1)}, u32[]{:S(2)}, u32[]{:S(2)}) collective-permute-start(bf16[4,80,768]{2,1,0:T(8,128)(2,1)S(1)} %get-tuple-element.327), channel_id=1, source_target_pairs={{0,2},{1,3},{2,0},{3,1},{4,6},{5,7},{6,4},{7,5},{8,10},{9,11},{10,... | collective-permute-start | bytes 1474568 | tf_op jit(solution)/shard_map/ppermute | solution.py:1010
  26.2 17.1 %collective-permute-start.4 = (bf16[4,80,768]{2,1,0:T(8,128)(2,1)S(1)}, bf16[4,80,768]{2,1,0:T(8,128)(2,1)S(1)}, u32[]{:S(2)}, u32[]{:S(2)}) collective-permute-start(bf16[4,80,768]{2,1,0:T(8,128)(2,1)S(1)} %get-tuple-element.326), channel_id=1, source_target_pairs={{0,4},{1,5},{2,6},{3,7},{4,0},{5,1},{6,2},{7,3},{8,12},{9,13},{10,... | collective-permute-start | bytes 1474568 | tf_op jit(solution)/shard_map/ppermute | solution.py:1010
  27.7 11.3 %collective-permute-start.5 = (bf16[176,384]{1,0:T(8,128)(2,1)S(1)}, bf16[176,384]{1,0:T(8,128)(2,1)S(1)}, u32[]{:S(2)}, u32[]{:S(2)}) collective-permute-start(bf16[176,384]{1,0:T(8,128)(2,1)S(1)} %pad_maximum_fusion.18), channel_id=1, source_target_pairs={{0,8},{1,9},{2,10},{3,11},{4,12},{5,13},{6,14},{7,15},{8,16},{9,17... | collective-permute-start | bytes 405512 | tf_op jit(solution)/shard_map/ppermute | solution.py:1023
  33.4 9.7 %collective-permute-start.6 = (bf16[176,384]{1,0:T(8,128)(2,1)S(1)}, bf16[176,384]{1,0:T(8,128)(2,1)S(1)}, u32[]{:S(2)}, u32[]{:S(2)}) collective-permute-start(bf16[176,384]{1,0:T(8,128)(2,1)S(1)} %pad_maximum_fusion.18), channel_id=1, source_target_pairs={{0,16},{1,17},{2,18},{3,19},{4,20},{5,21},{6,22},{7,23},{8,24},{9,... | collective-permute-start | bytes 405512 | tf_op jit(solution)/shard_map/ppermute | solution.py:1023
  35.0 8.1 %collective-permute-start.7 = (bf16[176,384]{1,0:T(8,128)(2,1)S(1)}, bf16[176,384]{1,0:T(8,128)(2,1)S(1)}, u32[]{:S(2)}, u32[]{:S(2)}) collective-permute-start(bf16[176,384]{1,0:T(8,128)(2,1)S(1)} %pad_maximum_fusion.18), channel_id=1, source_target_pairs={{0,24},{1,25},{2,26},{3,27},{4,28},{5,29},{6,30},{7,31},{8,0},{9,1... | collective-permute-start | bytes 405512 | tf_op jit(solution)/shard_map/ppermute | solution.py:1023
  43.4 32.0 %collective-permute-start.9 = (bf16[2,4,80,768]{3,2,1,0:T(8,128)(2,1)S(1)}, bf16[2,4,80,768]{3,2,1,0:T(8,128)(2,1)S(1)}, u32[]{:S(2)}, u32[]{:S(2)}) collective-permute-start(bf16[2,4,80,768]{3,2,1,0:T(8,128)(2,1)S(1)} %get-tuple-element.323), channel_id=1, source_target_pairs={{0,2},{1,3},{2,0},{3,1},{4,6},{5,7},{6,4},{7,5},{8,10},{9,11},{10,... | collective-permute-start | bytes 2949128 | tf_op jit(solution)/shard_map/ppermute | solution.py:1010
  44.1 31.3 %collective-permute-start.8 = (bf16[2,4,80,768]{3,2,1,0:T(8,128)(2,1)S(1)}, bf16[2,4,80,768]{3,2,1,0:T(8,128)(2,1)S(1)}, u32[]{:S(2)}, u32[]{:S(2)}) collective-permute-start(bf16[2,4,80,768]{3,2,1,0:T(8,128)(2,1)S(1)} %get-tuple-element.321), channel_id=1, source_target_pairs={{0,4},{1,5},{2,6},{3,7},{4,0},{5,1},{6,2},{7,3},{8,12},{9,13},{10,... | collective-permute-start | bytes 2949128 | tf_op jit(solution)/shard_map/ppermute | solution.py:1010
  44.7 12.6 %collective-permute-start.12 = (bf16[192,768]{1,0:T(8,128)(2,1)S(1)}, bf16[192,768]{1,0:T(8,128)(2,1)S(1)}, u32[]{:S(2)}, u32[]{:S(2)}) collective-permute-start(bf16[192,768]{1,0:T(8,128)(2,1)S(1)} %pad_maximum_fusion.11), channel_id=1, source_target_pairs={{0,8},{1,9},{2,10},{3,11},{4,12},{5,13},{6,14},{7,15},{8,16},{9,17... | collective-permute-start | bytes 884744 | tf_op jit(solution)/shard_map/ppermute | solution.py:1023
  48.1 19.5 %collective-permute-start.13 = (bf16[192,768]{1,0:T(8,128)(2,1)S(1)}, bf16[192,768]{1,0:T(8,128)(2,1)S(1)}, u32[]{:S(2)}, u32[]{:S(2)}) collective-permute-start(bf16[192,768]{1,0:T(8,128)(2,1)S(1)} %pad_maximum_fusion.11), channel_id=1, source_target_pairs={{0,16},{1,17},{2,18},{3,19},{4,20},{5,21},{6,22},{7,23},{8,24},{9,... | collective-permute-start | bytes 884744 | tf_op jit(solution)/shard_map/ppermute | solution.py:1023
  49.8 19.2 %collective-permute-start.14 = (bf16[192,768]{1,0:T(8,128)(2,1)S(1)}, bf16[192,768]{1,0:T(8,128)(2,1)S(1)}, u32[]{:S(2)}, u32[]{:S(2)}) collective-permute-start(bf16[192,768]{1,0:T(8,128)(2,1)S(1)} %pad_maximum_fusion.11), channel_id=1, source_target_pairs={{0,24},{1,25},{2,26},{3,27},{4,28},{5,29},{6,30},{7,31},{8,0},{9,1... | collective-permute-start | bytes 884744 | tf_op jit(solution)/shard_map/ppermute | solution.py:1023
  57.3 18.0 %collective-permute-start.10 = (bf16[4,96,384]{2,1,0:T(8,128)(2,1)S(1)}, bf16[4,96,384]{2,1,0:T(8,128)(2,1)S(1)}, u32[]{:S(2)}, u32[]{:S(2)}) collective-permute-start(bf16[4,96,384]{2,1,0:T(8,128)(2,1)S(1)} %get-tuple-element.333), channel_id=1, source_target_pairs={{0,2},{1,3},{2,0},{3,1},{4,6},{5,7},{6,4},{7,5},{8,10},{9,11},{10,... | collective-permute-start | bytes 884744 | tf_op jit(solution)/shard_map/ppermute | solution.py:1010
  67.6 7.8 %collective-permute-start.11 = (bf16[4,80,384]{2,1,0:T(8,128)(2,1)S(1)}, bf16[4,80,384]{2,1,0:T(8,128)(2,1)S(1)}, u32[]{:S(2)}, u32[]{:S(2)}) collective-permute-start(bf16[4,80,384]{2,1,0:T(8,128)(2,1)S(1)} %get-tuple-element.331), channel_id=1, source_target_pairs={{0,4},{1,5},{2,6},{3,7},{4,0},{5,1},{6,2},{7,3},{8,12},{9,13},{10,... | collective-permute-start | bytes 737288 | tf_op jit(solution)/shard_map/ppermute | solution.py:1010
  79.0 7.1 %collective-permute-start.15 = (bf16[16,160,768]{2,1,0:T(8,128)(2,1)}, bf16[16,160,768]{2,1,0:T(8,128)(2,1)}, u32[]{:S(2)}, u32[]{:S(2)}) collective-permute-start(bf16[16,160,768]{2,1,0:T(8,128)(2,1)} %bitcast.30.begin_own), channel_id=1, source_target_pairs={{0,1},{1,0},{2,3},{3,2},{4,5},{5,4},{6,7},{7,6},{8,9},{9,8},{10,11... | collective-permute-start | bytes 11796488 | tf_op jit(solution)/shard_map/ppermute | solution.py:1010
  80.3 28.7 %collective-permute-start.16 = (bf16[2,4,96,384]{3,2,1,0:T(8,128)(2,1)S(1)}, bf16[2,4,96,384]{3,2,1,0:T(8,128)(2,1)S(1)}, u32[]{:S(2)}, u32[]{:S(2)}) collective-permute-start(bf16[2,4,96,384]{3,2,1,0:T(8,128)(2,1)S(1)} %get-tuple-element.329), channel_id=1, source_target_pairs={{0,4},{1,5},{2,6},{3,7},{4,0},{5,1},{6,2},{7,3},{8,12},{9,13},{10,... | collective-permute-start | bytes 1769480 | tf_op jit(solution)/shard_map/ppermute | solution.py:1010
  83.0 25.9 %collective-permute-start.18 = (bf16[4,96,768]{2,1,0:T(8,128)(2,1)S(1)}, bf16[4,96,768]{2,1,0:T(8,128)(2,1)}, u32[]{:S(2)}, u32[]{:S(2)}) collective-permute-start(bf16[4,96,768]{2,1,0:T(8,128)(2,1)S(1)} %get-tuple-element.319), channel_id=1, source_target_pairs={{0,2},{1,3},{2,0},{3,1},{4,6},{5,7},{6,4},{7,5},{8,10},{9,11},{10,... | collective-permute-start | bytes 1769480 | tf_op jit(solution)/shard_map/ppermute | solution.py:1010
  84.5 24.5 %collective-permute-start.19 = (bf16[4,96,768]{2,1,0:T(8,128)(2,1)S(1)}, bf16[4,96,768]{2,1,0:T(8,128)(2,1)S(1)}, u32[]{:S(2)}, u32[]{:S(2)}) collective-permute-start(bf16[4,96,768]{2,1,0:T(8,128)(2,1)S(1)} %get-tuple-element.318), channel_id=1, source_target_pairs={{0,4},{1,5},{2,6},{3,7},{4,0},{5,1},{6,2},{7,3},{8,12},{9,13},{10,... | collective-permute-start | bytes 1769480 | tf_op jit(solution)/shard_map/ppermute | solution.py:1010
  85.1 23.8 %collective-permute-start.17 = (bf16[2,4,80,384]{3,2,1,0:T(8,128)(2,1)S(1)}, bf16[2,4,80,384]{3,2,1,0:T(8,128)(2,1)S(1)}, u32[]{:S(2)}, u32[]{:S(2)}) collective-permute-start(bf16[2,4,80,384]{3,2,1,0:T(8,128)(2,1)S(1)} %get-tuple-element.335), channel_id=1, source_target_pairs={{0,2},{1,3},{2,0},{3,1},{4,6},{5,7},{6,4},{7,5},{8,10},{9,11},{10,... | collective-permute-start | bytes 1474568 | tf_op jit(solution)/shard_map/ppermute | solution.py:1010
  111.7 28.4 %collective-permute-start.22 = (bf16[2,4,96,768]{3,2,1,0:T(8,128)(2,1)S(1)}, bf16[2,4,96,768]{3,2,1,0:T(8,128)(2,1)S(1)}, u32[]{:S(2)}, u32[]{:S(2)}) collective-permute-start(bf16[2,4,96,768]{3,2,1,0:T(8,128)(2,1)S(1)} %pad_maximum_fusion.4.down_first), channel_id=1, source_target_pairs={{0,2},{1,3},{2,0},{3,1},{4,6},{5,7},{6,4},{7,5},{8,10},{9,11},{10,... | collective-permute-start | bytes 3538952 | tf_op jit(solution)/shard_map/ppermute | solution.py:1010
  113.2 26.9 %collective-permute-start.24 = (bf16[2,4,96,768]{3,2,1,0:T(8,128)(2,1)S(1)}, bf16[2,4,96,768]{3,2,1,0:T(8,128)(2,1)S(1)}, u32[]{:S(2)}, u32[]{:S(2)}) collective-permute-start(bf16[2,4,96,768]{3,2,1,0:T(8,128)(2,1)S(1)} %pad_maximum_fusion.4.down_first), channel_id=1, source_target_pairs={{0,1},{1,0},{2,3},{3,2},{4,5},{5,4},{6,7},{7,6},{8,9},{9,8},{10,11... | collective-permute-start | bytes 3538952 | tf_op jit(solution)/shard_map/ppermute | solution.py:1010
  114.6 28.3 %collective-permute-start.21 = (bf16[2,4,96,768]{3,2,1,0:T(8,128)(2,1)S(1)}, bf16[2,4,96,768]{3,2,1,0:T(8,128)(2,1)S(1)}, u32[]{:S(2)}, u32[]{:S(2)}) collective-permute-start(bf16[2,4,96,768]{3,2,1,0:T(8,128)(2,1)S(1)} %pad_maximum_fusion.3.up_first), channel_id=1, source_target_pairs={{0,4},{1,5},{2,6},{3,7},{4,0},{5,1},{6,2},{7,3},{8,12},{9,13},{10,... | collective-permute-start | bytes 3538952 | tf_op jit(solution)/shard_map/ppermute | solution.py:1010
  115.9 27.0 %collective-permute-start.23 = (bf16[2,4,96,768]{3,2,1,0:T(8,128)(2,1)S(1)}, bf16[2,4,96,768]{3,2,1,0:T(8,128)(2,1)S(1)}, u32[]{:S(2)}, u32[]{:S(2)}) collective-permute-start(bf16[2,4,96,768]{3,2,1,0:T(8,128)(2,1)S(1)} %pad_maximum_fusion.3.up_first), channel_id=1, source_target_pairs={{0,1},{1,0},{2,3},{3,2},{4,5},{5,4},{6,7},{7,6},{8,9},{9,8},{10,11... | collective-permute-start | bytes 3538952 | tf_op jit(solution)/shard_map/ppermute | solution.py:1010
  166.8 22.0 %collective-permute-start.27 = (bf16[512,4608]{1,0:T(8,128)(2,1)}, bf16[512,4608]{1,0:T(8,128)(2,1)}, u32[]{:S(2)}, u32[]{:S(2)}) collective-permute-start(bf16[512,4608]{1,0:T(8,128)(2,1)} %get-tuple-element.183.rows), channel_id=1, source_target_pairs={{0,1},{1,0},{2,3},{3,2},{4,5},{5,4},{6,7},{7,6},{8,9},{9,8},{10,11... | collective-permute-start | bytes 14155784 | tf_op jit(solution)/shard_map/ppermute | solution.py:1010
  188.8 10.8 %collective-permute-start.28 = (bf16[2992,768]{1,0:T(8,128)(2,1)}, bf16[2992,768]{1,0:T(8,128)(2,1)S(1)}, u32[]{:S(2)}, u32[]{:S(2)}) collective-permute-start(bf16[2992,768]{1,0:T(8,128)(2,1)} %get-tuple-element.184), channel_id=1, source_target_pairs={{0,1},{1,0},{2,3},{3,2},{4,5},{5,4},{6,7},{7,6},{8,9},{9,8},{10,11... | collective-permute-start | bytes 13787144 | tf_op jit(solution)/shard_map/ppermute | solution.py:1010
  199.6 28.1 %collective-permute-start.29 = (bf16[2,4,96,768]{3,2,1,0:T(8,128)(2,1)S(1)}, bf16[2,4,96,768]{3,2,1,0:T(8,128)(2,1)S(1)}, u32[]{:S(2)}, u32[]{:S(2)}) collective-permute-start(bf16[2,4,96,768]{3,2,1,0:T(8,128)(2,1)S(1)} %get-tuple-element.196), channel_id=1, source_target_pairs={{0,4},{1,5},{2,6},{3,7},{4,0},{5,1},{6,2},{7,3},{8,12},{9,13},{10,... | collective-permute-start | bytes 3538952 | tf_op jit(solution)/shard_map/ppermute | solution.py:1010
  200.9 27.7 %collective-permute-start.30 = (bf16[2,4,96,768]{3,2,1,0:T(8,128)(2,1)S(1)}, bf16[2,4,96,768]{3,2,1,0:T(8,128)(2,1)S(1)}, u32[]{:S(2)}, u32[]{:S(2)}) collective-permute-start(bf16[2,4,96,768]{3,2,1,0:T(8,128)(2,1)S(1)} %get-tuple-element.197), channel_id=1, source_target_pairs={{0,2},{1,3},{2,0},{3,1},{4,6},{5,7},{6,4},{7,5},{8,10},{9,11},{10,... | collective-permute-start | bytes 3538952 | tf_op jit(solution)/shard_map/ppermute | solution.py:1010
  228.6 21.7 %collective-permute-start.32 = (bf16[2,4,72,768]{3,2,1,0:T(8,128)(2,1)S(1)}, bf16[2,4,72,768]{3,2,1,0:T(8,128)(2,1)S(1)}, u32[]{:S(2)}, u32[]{:S(2)}) collective-permute-start(bf16[2,4,72,768]{3,2,1,0:T(8,128)(2,1)S(1)} %get-tuple-element.208), channel_id=1, source_target_pairs={{0,2},{1,3},{2,0},{3,1},{4,6},{5,7},{6,4},{7,5},{8,10},{9,11},{10,... | collective-permute-start | bytes 2654216 | tf_op jit(solution)/shard_map/ppermute | solution.py:1010
  229.4 21.0 %collective-permute-start.31 = (bf16[2,4,64,768]{3,2,1,0:T(8,128)(2,1)S(1)}, bf16[2,4,64,768]{3,2,1,0:T(8,128)(2,1)S(1)}, u32[]{:S(2)}, u32[]{:S(2)}) collective-permute-start(bf16[2,4,64,768]{3,2,1,0:T(8,128)(2,1)S(1)} %get-tuple-element.207), channel_id=1, source_target_pairs={{0,4},{1,5},{2,6},{3,7},{4,0},{5,1},{6,2},{7,3},{8,12},{9,13},{10,... | collective-permute-start | bytes 2359304 | tf_op jit(solution)/shard_map/ppermute | solution.py:1010
  250.6 16.2 %collective-permute-start.34 = (bf16[4,96,768]{2,1,0:T(8,128)(2,1)S(1)}, bf16[4,96,768]{2,1,0:T(8,128)(2,1)S(1)}, u32[]{:S(2)}, u32[]{:S(2)}) collective-permute-start(bf16[4,96,768]{2,1,0:T(8,128)(2,1)S(1)} %fusion), channel_id=1, source_target_pairs={{0,2},{1,3},{2,0},{3,1},{4,6},{5,7},{6,4},{7,5},{8,10},{9,11},{10,... | collective-permute-start | bytes 1769480 | tf_op jit(solution)/shard_map/ppermute | solution.py:1010
  252.1 16.5 %collective-permute-start.35 = (bf16[4,96,768]{2,1,0:T(8,128)(2,1)S(1)}, bf16[4,96,768]{2,1,0:T(8,128)(2,1)S(1)}, u32[]{:S(2)}, u32[]{:S(2)}) collective-permute-start(bf16[4,96,768]{2,1,0:T(8,128)(2,1)S(1)} %fusion.1), channel_id=1, source_target_pairs={{0,4},{1,5},{2,6},{3,7},{4,0},{5,1},{6,2},{7,3},{8,12},{9,13},{10,... | collective-permute-start | bytes 1769480 | tf_op jit(solution)/shard_map/ppermute | solution.py:1010
  256.4 25.7 %collective-permute-start.39 = (bf16[4,72,768]{2,1,0:T(8,128)(2,1)S(1)}, bf16[4,72,768]{2,1,0:T(8,128)(2,1)S(1)}, u32[]{:S(2)}, u32[]{:S(2)}) collective-permute-start(bf16[4,72,768]{2,1,0:T(8,128)(2,1)S(1)} %fusion.4), channel_id=1, source_target_pairs={{0,4},{1,5},{2,6},{3,7},{4,0},{5,1},{6,2},{7,3},{8,12},{9,13},{10,... | collective-permute-start | bytes 1327112 | tf_op jit(solution)/shard_map/ppermute | solution.py:1010
  257.7 24.3 %collective-permute-start.38 = (bf16[4,64,768]{2,1,0:T(8,128)(2,1)S(1)}, bf16[4,64,768]{2,1,0:T(8,128)(2,1)S(1)}, u32[]{:S(2)}, u32[]{:S(2)}) collective-permute-start(bf16[4,64,768]{2,1,0:T(8,128)(2,1)S(1)} %fusion.7), channel_id=1, source_target_pairs={{0,2},{1,3},{2,0},{3,1},{4,6},{5,7},{6,4},{7,5},{8,10},{9,11},{10,... | collective-permute-start | bytes 1179656 | tf_op jit(solution)/shard_map/ppermute | solution.py:1010
  268.8 13.3 %collective-permute-start.40 = (bf16[192,768]{1,0:T(8,128)(2,1)S(1)}, bf16[192,768]{1,0:T(8,128)(2,1)S(1)}, u32[]{:S(2)}, u32[]{:S(2)}) collective-permute-start(bf16[192,768]{1,0:T(8,128)(2,1)S(1)} %pad_maximum_fusion.12), channel_id=1, source_target_pairs={{0,8},{1,9},{2,10},{3,11},{4,12},{5,13},{6,14},{7,15},{8,16},{9,17... | collective-permute-start | bytes 884744 | tf_op jit(solution)/shard_map/ppermute | solution.py:1023
  279.3 16.6 %collective-permute-start.37 = (bf16[2,4,56,768]{3,2,1,0:T(8,128)(2,1)S(1)}, bf16[2,4,56,768]{3,2,1,0:T(8,128)(2,1)S(1)}, u32[]{:S(2)}, u32[]{:S(2)}) collective-permute-start(bf16[2,4,56,768]{3,2,1,0:T(8,128)(2,1)S(1)} %get-tuple-element.224), channel_id=1, source_target_pairs={{0,2},{1,3},{2,0},{3,1},{4,6},{5,7},{6,4},{7,5},{8,10},{9,11},{10,... | collective-permute-start | bytes 2064392 | tf_op jit(solution)/shard_map/ppermute | solution.py:1010
  280.4 12.9 %collective-permute-start.36 = (bf16[2,4,48,768]{3,2,1,0:T(8,128)(2,1)S(1)}, bf16[2,4,48,768]{3,2,1,0:T(8,128)(2,1)S(1)}, u32[]{:S(2)}, u32[]{:S(2)}) collective-permute-start(bf16[2,4,48,768]{3,2,1,0:T(8,128)(2,1)S(1)} %get-tuple-element.223), channel_id=1, source_target_pairs={{0,4},{1,5},{2,6},{3,7},{4,0},{5,1},{6,2},{7,3},{8,12},{9,13},{10,... | collective-permute-start | bytes 1769480 | tf_op jit(solution)/shard_map/ppermute | solution.py:1010
  282.1 13.7 %collective-permute-start.42 = (bf16[192,768]{1,0:T(8,128)(2,1)S(1)}, bf16[192,768]{1,0:T(8,128)(2,1)S(1)}, u32[]{:S(2)}, u32[]{:S(2)}) collective-permute-start(bf16[192,768]{1,0:T(8,128)(2,1)S(1)} %fusion.2), channel_id=1, source_target_pairs={{0,8},{1,9},{2,10},{3,11},{4,12},{5,13},{6,14},{7,15},{8,16},{9,17... | collective-permute-start | bytes 884744 | tf_op jit(solution)/shard_map/ppermute | solution.py:1023
  283.1 12.8 %collective-permute-start.41 = (bf16[136,768]{1,0:T(8,128)(2,1)S(1)}, bf16[136,768]{1,0:T(8,128)(2,1)S(1)}, u32[]{:S(2)}, u32[]{:S(2)}) collective-permute-start(bf16[136,768]{1,0:T(8,128)(2,1)S(1)} %pad_maximum_fusion.13), channel_id=1, source_target_pairs={{0,8},{1,9},{2,10},{3,11},{4,12},{5,13},{6,14},{7,15},{8,16},{9,17... | collective-permute-start | bytes 626696 | tf_op jit(solution)/shard_map/ppermute | solution.py:1023
  295.9 12.8 %collective-permute-start.46 = (bf16[192,768]{1,0:T(8,128)(2,1)S(1)}, bf16[192,768]{1,0:T(8,128)(2,1)S(1)}, u32[]{:S(2)}, u32[]{:S(2)}) collective-permute-start(bf16[192,768]{1,0:T(8,128)(2,1)S(1)} %fusion.3), channel_id=1, source_target_pairs={{0,8},{1,9},{2,10},{3,11},{4,12},{5,13},{6,14},{7,15},{8,16},{9,17... | collective-permute-start | bytes 884744 | tf_op jit(solution)/shard_map/ppermute | solution.py:1023
  296.1 12.7 %collective-permute-start.44 = (bf16[4,56,768]{2,1,0:T(8,128)(2,1)S(1)}, bf16[4,56,768]{2,1,0:T(8,128)(2,1)S(1)}, u32[]{:S(2)}, u32[]{:S(2)}) collective-permute-start(bf16[4,56,768]{2,1,0:T(8,128)(2,1)S(1)} %fusion.8), channel_id=1, source_target_pairs={{0,4},{1,5},{2,6},{3,7},{4,0},{5,1},{6,2},{7,3},{8,12},{9,13},{10,... | collective-permute-start | bytes 1032200 | tf_op jit(solution)/shard_map/ppermute | solution.py:1010
  297.5 11.3 %collective-permute-start.43 = (bf16[4,48,768]{2,1,0:T(8,128)(2,1)S(1)}, bf16[4,48,768]{2,1,0:T(8,128)(2,1)S(1)}, u32[]{:S(2)}, u32[]{:S(2)}) collective-permute-start(bf16[4,48,768]{2,1,0:T(8,128)(2,1)S(1)} %fusion.11), channel_id=1, source_target_pairs={{0,2},{1,3},{2,0},{3,1},{4,6},{5,7},{6,4},{7,5},{8,10},{9,11},{10,... | collective-permute-start | bytes 884744 | tf_op jit(solution)/shard_map/ppermute | solution.py:1010
  298.2 10.6 %collective-permute-start.45 = (bf16[136,768]{1,0:T(8,128)(2,1)S(1)}, bf16[136,768]{1,0:T(8,128)(2,1)S(1)}, u32[]{:S(2)}, u32[]{:S(2)}) collective-permute-start(bf16[136,768]{1,0:T(8,128)(2,1)S(1)} %fusion.5), channel_id=1, source_target_pairs={{0,8},{1,9},{2,10},{3,11},{4,12},{5,13},{6,14},{7,15},{8,16},{9,17... | collective-permute-start | bytes 626696 | tf_op jit(solution)/shard_map/ppermute | solution.py:1023
  308.8 18.3 %collective-permute-start.47 = (bf16[136,768]{1,0:T(8,128)(2,1)S(1)}, bf16[136,768]{1,0:T(8,128)(2,1)S(1)}, u32[]{:S(2)}, u32[]{:S(2)}) collective-permute-start(bf16[136,768]{1,0:T(8,128)(2,1)S(1)} %fusion.6), channel_id=1, source_target_pairs={{0,8},{1,9},{2,10},{3,11},{4,12},{5,13},{6,14},{7,15},{8,16},{9,17... | collective-permute-start | bytes 626696 | tf_op jit(solution)/shard_map/ppermute | solution.py:1023
  309.2 8.6 %collective-permute-start.48 = (bf16[104,768]{1,0:T(8,128)(2,1)S(1)}, bf16[104,768]{1,0:T(8,128)(2,1)S(1)}, u32[]{:S(2)}, u32[]{:S(2)}) collective-permute-start(bf16[104,768]{1,0:T(8,128)(2,1)S(1)} %pad_maximum_fusion.14), channel_id=1, source_target_pairs={{0,24},{1,25},{2,26},{3,27},{4,28},{5,29},{6,30},{7,31},{8,0},{9,1... | collective-permute-start | bytes 479240 | tf_op jit(solution)/shard_map/ppermute | solution.py:1023
  313.1 13.8 %collective-permute-start.49 = (bf16[104,768]{1,0:T(8,128)(2,1)S(1)}, bf16[104,768]{1,0:T(8,128)(2,1)S(1)}, u32[]{:S(2)}, u32[]{:S(2)}) collective-permute-start(bf16[104,768]{1,0:T(8,128)(2,1)S(1)} %pad_maximum_fusion.15), channel_id=1, source_target_pairs={{0,16},{1,17},{2,18},{3,19},{4,20},{5,21},{6,22},{7,23},{8,24},{9,... | collective-permute-start | bytes 479240 | tf_op jit(solution)/shard_map/ppermute | solution.py:1023
  313.2 13.7 %collective-permute-start.50 = (bf16[104,768]{1,0:T(8,128)(2,1)S(1)}, bf16[104,768]{1,0:T(8,128)(2,1)S(1)}, u32[]{:S(2)}, u32[]{:S(2)}) collective-permute-start(bf16[104,768]{1,0:T(8,128)(2,1)S(1)} %pad_maximum_fusion.16), channel_id=1, source_target_pairs={{0,8},{1,9},{2,10},{3,11},{4,12},{5,13},{6,14},{7,15},{8,16},{9,17... | collective-permute-start | bytes 479240 | tf_op jit(solution)/shard_map/ppermute | solution.py:1023
  332.7 9.8 %all-to-all-start = ((f32[32,2,128]{2,1,0:T(2,128)}), f32[32,2,128]{2,1,0:T(2,128)S(1)}, u32[]{:S(2)}, u32[]{:S(2)}) async-start(f32[32,2,128]{2,1,0:T(2,128)} %broadcast_in_dim.18), calls=%async_computation | async-start | bytes 65536 | tf_op jit(solution)/shard_map/all_to_all | solution.py:1767
  (80 other events, 550.3 us)
